TPU v7x, 256 devices: a whole 4x4x8 slice. The times are simulated.
256 devices in a mesh: tok: 16 (over x, y_lo, core), ch: 16 (over y_hi, z).
Axes of the slice: x: 4, y: 4 (y_hi: 2, y_lo: 2; y = y_hi * 2 + y_lo), z: 8, core: 2. Of those that a mesh axis runs over, the one named last changes fastest.
Arguments:
- activations: bfloat16 [4096, 8192], P('tok', 'ch'), may hold values from -25 to 25
- weight: bfloat16 [14336, 8192], P('tok', 'ch'), may hold values from -0.0625 to 0.0625
- basis: bfloat16 [1024, 8192], P(None, 'ch'), may hold values from -0.0625 to 0.0625
Outputs:
- left_factor: float32 [14336, 1024], P(('tok', 'ch'))
All inputs are finite; a program needn't handle non-finite values.
Results may differ from a plain program's by a relative error of at most 0.0088.
Values sent between devices are 32-bit elements; how exact they have to be, the bound alone decides.
No kernel may reach another device: no remote copies, remote signals or barrier semaphores. Data moves between devices by JAX's collectives and lax.ppermute only.
A program may use at most 128 MiB of HBM per device.

v0:
```python
import jax
import jax.numpy as jnp
from jax import lax
from jax.sharding import PartitionSpec as P

damping = 0.1


def shards(activations, weight, basis):
    partial_value = lax.dot_general(
        activations, basis, (((1,), (1,)), ((), ())), preferred_element_type=jnp.float32
    )
    codes = lax.psum(partial_value, "ch")
    rank_width = codes.shape[1]
    channels = lax.axis_size("ch")
    column_width = rank_width // channels
    own_columns = lax.dynamic_slice_in_dim(
        codes, lax.axis_index("ch") * column_width, column_width, 1
    )
    columns = lax.dot_general(
        codes,
        own_columns,
        (((0,), (0,)), ((), ())),
        precision=lax.Precision.HIGHEST,
        preferred_element_type=jnp.float32,
    )
    summed = lax.psum(columns, "tok")
    gram = lax.all_gather(summed, "ch", axis=1, tiled=True)
    codes_low = codes.astype(jnp.bfloat16)
    local_moments = lax.dot_general(
        activations, codes_low, (((0,), (0,)), ((), ())), preferred_element_type=jnp.float32
    )
    moments = lax.psum(local_moments, "tok")
    rows_part = weight.astype(jnp.float32)
    cross = lax.psum_scatter(
        jnp.dot(
            rows_part, moments, precision=lax.Precision.HIGHEST, preferred_element_type=jnp.float32
        ),
        "ch",
        scatter_dimension=0,
        tiled=True,
    )
    ridge = damping * jnp.trace(gram) / rank_width
    damped = gram + ridge * jnp.eye(rank_width, dtype=jnp.float32)
    lower = jnp.linalg.cholesky(damped)
    middle = jax.scipy.linalg.solve_triangular(lower, cross.T, lower=True)
    solved = jax.scipy.linalg.solve_triangular(lower, middle, trans=1, lower=True)
    return solved.T


def solution(mesh):
    in_specs = (P("tok", "ch"), P("tok", "ch"), P(None, "ch"))
    out_specs = P(("tok", "ch"), None)
    return jax.shard_map(shards, mesh=mesh, in_specs=in_specs, out_specs=out_specs, check_vma=False)
```

profile of v0, /device:TPU:1, one launch (start us, length us, event | category | flops | bytes accessed | tf_op | source)
XLA Modules:
  0.0 987.1 jit_solution(12627589601569377898)
XLA Ops:
  10.2 152.5 %all-reduce.5.cloned.1.call-done = f32[256,1024]{1,0:T(8,128)} async-done(((f32[256,1024]{1,0:T(8,128)}), f32[256,1024]{1,0:T(8,128)}) %all-reduce.5.cloned.1.call-update) | async-done | bytes 1048592 | tf_op jit(solution)/shard_map/psum | solution.py:13
  162.7 3.1 convolution_bitcast_fusion.1
  168.7 137.0 %all-reduce.7.cloned.1.call-done = (f32[512,1024]{0,1:T(8,128)}, f32[1024,64]{0,1:T(8,128)}) async-done(((f32[512,1024]{0,1:T(8,128)}, f32[1024,64]{0,1:T(8,128)}), (f32[512,1024]{0,1:T(8,128)}, f32[1024,64]{0,1:T(8,128)})) %all-reduce.7.cloned.1.call-update) | async-done | bytes 2359312 | tf_op jit(solution)/shard_map/psum | solution.py:33
  305.6 6.9 convolution_bitcast_fusion
  312.5 5.0 copy.44
  318.2 208.6 %reduce-scatter.4.cloned.1.call-done = f32[56,1024]{1,0:T(8,128)} async-done(((f32[896,1024]{1,0:T(8,128)}), f32[56,1024]{1,0:T(8,128)}) %reduce-scatter.4.cloned.1.call-update) | async-done | bytes 229392
  527.9 99.8 %all-gather.2.cloned.1.call-done = f32[1024,1024]{0,1:T(8,128)} async-done(((f32[1024,64]{0,1:T(8,128)}), f32[1024,1024]{0,1:T(8,128)}) %all-gather.2.cloned.1.call-update) | async-done | bytes 4194320 | tf_op jit(solution)/shard_map/all_gather | solution.py:28
  627.6 2.9 select_reduce_fusion
  631.2 4.8 select_add_fusion
  636.0 5.8 copy.21
  641.8 4.5 fusion
  648.2 11.7 %cholesky.222 = f32[128,128]{1,0:T(8,128)S(1)} custom-call(f32[128,128]{1,0:T(8,128)S(1)} %cholesky.577), custom_call_target="Cholesky" | custom-call | tf_op jit(solution)/shard_map/jit(cholesky)/cholesky | solution.py:45
  660.1 9.8 custom-call.66
  673.2 11.7 %cholesky.243 = f32[128,128]{1,0:T(8,128)S(1)} custom-call(f32[128,128]{1,0:T(8,128)S(1)} %cholesky.581), custom_call_target="Cholesky" | custom-call | tf_op jit(solution)/shard_map/jit(cholesky)/cholesky | solution.py:45
  685.2 9.8 custom-call.67
  700.5 11.7 %cholesky.466 = f32[128,128]{1,0:T(8,128)S(1)} custom-call(f32[128,128]{1,0:T(8,128)S(1)} %cholesky.586), custom_call_target="Cholesky" | custom-call | tf_op jit(solution)/shard_map/jit(cholesky)/cholesky | solution.py:45
  713.0 9.8 custom-call.68
  724.1 3.3 convolution_subtract_fusion.2
  727.5 11.7 %cholesky.485 = f32[128,128]{1,0:T(8,128)S(1)} custom-call(f32[128,128]{1,0:T(8,128)S(1)} %cholesky.591), custom_call_target="Cholesky" | custom-call | tf_op jit(solution)/shard_map/jit(cholesky)/cholesky | solution.py:45
  739.9 9.8 custom-call.69
  750.9 3.1 convolution_subtract_fusion.3
  754.1 12.1 %cholesky.504 = f32[128,128]{1,0:T(8,128)S(1)} custom-call(f32[128,128]{1,0:T(8,128)S(1)} %cholesky.596), custom_call_target="Cholesky" | custom-call | tf_op jit(solution)/shard_map/jit(cholesky)/cholesky | solution.py:45
  766.9 9.8 custom-call.70
  777.9 3.1 convolution_subtract_fusion.4
  780.9 11.7 %cholesky.524 = f32[128,128]{1,0:T(8,128)S(1)} custom-call(f32[128,128]{1,0:T(8,128)S(1)} %cholesky.601), custom_call_target="Cholesky" | custom-call | tf_op jit(solution)/shard_map/jit(cholesky)/cholesky | solution.py:45
  793.4 9.8 custom-call.71
  807.1 11.7 %cholesky.544 = f32[128,128]{1,0:T(8,128)S(1)} custom-call(f32[128,128]{1,0:T(8,128)S(1)} %cholesky.606), custom_call_target="Cholesky" | custom-call | tf_op jit(solution)/shard_map/jit(cholesky)/cholesky | solution.py:45
  819.6 9.8 custom-call.72
  832.4 11.7 %cholesky.562 = f32[128,128]{1,0:T(8,128)S(1)} custom-call(f32[128,128]{1,0:T(8,128)S(1)} %convolution_subtract_fusion.10), custom_call_target="Cholesky" | custom-call | tf_op jit(solution)/shard_map/jit(cholesky)/cholesky | solution.py:45
  854.6 4.8 select_select_fusion
  859.4 23.7 %while.1 = (s32[]{:T(128)}, f32[1024,1024]{0,1:T(8,128)}, s32[8,2]{0,1:T(2,128)S(1)}, f32[8,128,128]{2,1,0:T(8,128)S(1)}, s32[]{:T(128)}) while((s32[]{:T(128)}, f32[1024,1024]{0,1:T(8,128)}, s32[8,2]{0,1:T(2,128)S(1)}, f32[8,128,128]{2,1,0:T(8,128)S(1)}, s32[]{:T(128)}) %tuple.50), condition=%wide.while_cond, body=%wide.while_body.sunk | while | flops 2 | bytes 393329 | solution.py:47
  883.2 78.8 %custom-call.73 = f32[8,128,128]{1,2,0:T(8,128)S(1)} custom-call(f32[8,128,128]{2,1,0:T(8,128)S(1)} %get-tuple-element.12), custom_call_target="InvertDiagBlocksLowerTriangular" | custom-call | tf_op jit(solution)/shard_map/jit(_solve_triangular)/triangular_solve | solution.py:47
  (169 shorter events, 80.5 us)
Async XLA Ops:
  6.5 1.2 copy-start
  6.5 156.2 %all-reduce.5.cloned.1.call-start = ((), (), s32[]{:S(2)}) async-start(), calls=%async_computation.1 | async-start | bytes 2097152 | tf_op jit(solution)/shard_map/psum | solution.py:13
  10.2 295.5 %copy-start.4 = (bf16[896,512]{1,0:T(8,128)(2,1)S(1)}, bf16[896,512]{1,0:T(8,128)(2,1)}, u32[]{:S(2)}) copy-start(bf16[896,512]{1,0:T(8,128)(2,1)} %param.4) | copy-start | bytes 2752516
  10.2 295.4 %all-reduce.7.cloned.1.call-start = ((), (), s32[]{:S(2)}) async-start(), calls=%async_computation.4 | async-start | bytes 4718592 | tf_op jit(solution)/shard_map/psum | solution.py:33
  168.6 358.1 %reduce-scatter.4.cloned.1.call-start = ((), (), s32[]{:S(2)}) async-start(), calls=%async_computation.3 | async-start | bytes 3899392
  317.6 310.1 %all-gather.2.cloned.1.call-start = ((), (), s32[]{:S(2)}) async-start(), calls=%async_computation.2 | async-start | bytes 4456448 | tf_op jit(solution)/shard_map/all_gather | solution.py:28
  646.3 1.9 copy-start.3
  696.1 2.0 copy-start.1
  962.0 11.0 %copy-start.2 = (f32[1024,1024]{0,1:T(8,128)S(1)}, f32[1024,1024]{0,1:T(8,128)}, u32[]{:S(2)}) copy-start(f32[1024,1024]{0,1:T(8,128)} %get-tuple-element.132) | copy-start | bytes 12582916
  979.6 0.7 copy-start.5
Sparse Core Ops, SparseCore 0:
  10.3 152.3 all-reduce.4
  168.7 136.8 all-reduce.6
  317.7 209.0 reduce-scatter.3
  529.2 98.4 all-gather.1
where the time goes:
time: 996 us; the launch traced here: 987 us
  waiting for transfers between devices  598 us (60%)
  other arithmetic  264 us (27%)
  matrix products  58.2 us (6%)
  local copies, waits for them, and re-layouts  46.9 us (5%)
  between operations  19.7 us (2%)
    unnamed x5, waiting for transfers between devices  209 us
    another operation x30, other arithmetic, shards(): lower = jnp.linalg.cholesky(damped)  168 us
    psum x1, waiting for transfers between devices, shards(): codes = lax.psum(partial_value, 'ch')  152 us
    psum x1, waiting for transfers between devices, shards(): moments = lax.psum(local_moments, 'tok')  137 us
    all_gather x1, waiting for transfers between devices, shards(): gram = lax.all_gather(summed, 'ch', axis=1, tiled=True)  99.8 us
    another operation x3, other arithmetic, shards(): jax.scipy.linalg.solve_triangular(lower, middle, trans=1, lower=True)  83.6 us
    another operation x14, matrix products, shards(): lower = jnp.linalg.cholesky(damped)  25.9 us
    another operation x40, local copies, waits for them, and re-layouts  23.5 us
  transfers between devices with their start and end apart: 4, of which 4 were waited for; matrix products, arithmetic and copies ran while one was open for 0% of the time, Pallas kernels for 0%

commit v1 on v0

v1 whole, which is shorter than its diff:
```python
import jax
import jax.numpy as jnp
from jax import lax
from jax.experimental import pallas as pl
from jax.experimental.pallas import tpu as pltpu
from jax.sharding import Mesh
from jax.sharding import PartitionSpec as P

damping = 0.1

SUB, LANE = 8, 128
AXES = (("x", 4), ("y_lo", 2), ("core", 2), ("y_hi", 2), ("z", 8))
TOK = ("x", "y_lo", "core")
PLANE = ("x", "y_lo")
CH = ("y_hi", "z")


def tree_sum(terms):
    while len(terms) > 1:
        paired = [a + b for a, b in zip(terms[::2], terms[1::2])]
        terms = paired + ([terms[-1]] if len(terms) % 2 else [])
    return terms[0]


def spread(value):
    return jnp.broadcast_to(value, (SUB, LANE))


def invert_small(entry):
    for k in range(SUB):
        inverse = 1.0 / entry[k, k]
        row = [entry[min(k, j), max(k, j)] for j in range(SUB)]
        scaled = [value * inverse for value in row]
        for i in range(SUB):
            for j in range(i, SUB):
                if i != k and j != k:
                    entry[i, j] = entry[i, j] - scaled[i] * row[j]
        for j in range(SUB):
            if j != k:
                entry[min(k, j), max(k, j)] = scaled[j]
        entry[k, k] = -inverse
    return {place: -value for place, value in entry.items()}


def invert_block(block, between=None):
    sub = lax.broadcasted_iota(jnp.int32, (SUB, LANE), 0)
    lane = lax.broadcasted_iota(jnp.int32, (SUB, LANE), 1)
    panels = LANE // SUB
    rows = [block[r * SUB : (r + 1) * SUB, :] for r in range(panels)]
    for p in range(panels):
        base = p * SUB
        panel = rows[p]
        inside = (lane >= base) & (lane < base + SUB)
        columns = [spread(panel[:, base + j : base + j + 1]) for j in range(SUB)]
        small = invert_small(
            {(i, j): spread(columns[j][i : i + 1, :]) for j in range(SUB) for i in range(j + 1)}
        )
        small_columns = []
        for j in range(SUB):
            column = small[0, j]
            for i in range(1, SUB):
                column = jnp.where(sub == i, small[min(i, j), max(i, j)], column)
            small_columns.append(column)
        wide = jnp.where(inside, jnp.where(lane - base == sub, 1.0, 0.0), panel)
        pivot = tree_sum([small_columns[j] * spread(wide[j : j + 1, :]) for j in range(SUB)])
        pivot_rows = [spread(pivot[j : j + 1, :]) for j in range(SUB)]
        for r in list(range(p + 1, panels)) + list(range(p)):
            change = tree_sum(
                [spread(rows[r][:, base + j : base + j + 1]) * pivot_rows[j] for j in range(SUB)]
            )
            rows[r] = jnp.where(inside, 0.0, rows[r]) - change
        rows[p] = pivot
        if between is not None:
            between(p)
    return rows


def split(value):
    high = value.astype(jnp.bfloat16)
    rest = value - high.astype(jnp.float32)
    middle = rest.astype(jnp.bfloat16)
    low = (rest - middle.astype(jnp.float32)).astype(jnp.bfloat16)
    return high, middle, low


def left_parts(value):
    high, middle, low = split(value)
    return jnp.concatenate([high, middle, high, middle, high, low], 1)


def right_parts(value):
    high, middle, low = split(value)
    return jnp.concatenate([high, high, middle, middle, low, high], 0)


def product(left, right):
    return jnp.dot(left, right, preferred_element_type=jnp.float32)


def inverse_kernel(gram_ref, out_ref, left_ref, right_ref, block_ref):
    size = gram_ref.shape[0]
    blocks = size // LANE
    tile = 256
    row = lax.broadcasted_iota(jnp.int32, (LANE, LANE), 0)
    column = lax.broadcasted_iota(jnp.int32, (LANE, LANE), 1)
    diagonal = row == column
    total = jnp.zeros((LANE, LANE), jnp.float32)
    for b in range(blocks):
        own = slice(b * LANE, (b + 1) * LANE)
        total = total + jnp.where(diagonal, gram_ref[own, own], 0.0)
    ridge = damping * jnp.sum(total) / size
    out_ref[...] = gram_ref[...]
    for b in range(blocks):
        own = slice(b * LANE, (b + 1) * LANE)
        out_ref[own, own] = gram_ref[own, own] + jnp.where(diagonal, ridge, 0.0)

    def keep(rows):
        for r in range(LANE // SUB):
            block_ref[r * SUB : (r + 1) * SUB, :] = rows[r]

    keep(invert_block(out_ref[0:LANE, 0:LANE]))

    def step(k, carry):
        here = pl.ds(pl.multiple_of(k * LANE, LANE), LANE)
        after = pl.ds(pl.multiple_of(lax.rem(k + 1, blocks) * LANE, LANE), LANE)
        inverse = block_ref[...]
        inverse_parts = left_parts(inverse)
        ahead = product(inverse_parts, right_parts(out_ref[here, after]))
        following = out_ref[after, after] - product(
            left_parts(out_ref[after, here]), right_parts(ahead)
        )
        for m in range(blocks):
            rows = slice(m * LANE, (m + 1) * LANE)
            left_ref[rows, :] = left_parts(out_ref[rows, here])
        left_ref[here, :] = jnp.zeros((LANE, 6 * LANE), jnp.bfloat16)
        for m in range(size // tile):
            columns = slice(m * tile, (m + 1) * tile)
            scaled = product(inverse_parts, right_parts(out_ref[here, columns]))
            right_ref[:, columns] = right_parts(scaled)
            out_ref[here, columns] = scaled
        out_ref[:, here] = jnp.zeros((size, LANE), jnp.float32)
        out_ref[here, here] = inverse
        right_ref[:, here] = right_parts(inverse)

        def update(p):
            n, m = divmod(p, size // tile)
            columns = slice(n * tile, (n + 1) * tile)
            rows = slice(m * tile, (m + 1) * tile)
            out_ref[rows, columns] = out_ref[rows, columns] - product(
                left_ref[rows, :], right_ref[:, columns]
            )

        keep(invert_block(following, update))
        return carry

    lax.fori_loop(0, blocks, step, 0)


def damped_inverse(gram):
    size = gram.shape[0]
    return pl.pallas_call(
        inverse_kernel,
        out_shape=jax.ShapeDtypeStruct((size, size), jnp.float32),
        scratch_shapes=[
            pltpu.VMEM((size, 6 * LANE), jnp.bfloat16),
            pltpu.VMEM((6 * LANE, size), jnp.bfloat16),
            pltpu.VMEM((LANE, LANE), jnp.float32),
        ],
        compiler_params=pltpu.CompilerParams(vmem_limit_bytes=40 * 2**20),
        cost_estimate=pl.CostEstimate(
            flops=12 * size**3, bytes_accessed=8 * size**2, transcendentals=0
        ),
    )(gram)


def exchange_sum(value, axes, count):
    received = lax.all_to_all(value, axes, 0, 0, tiled=True)
    return received.reshape(count, -1, value.shape[1]).sum(0)


def exchange_gather(value, axes, count):
    copies = jnp.broadcast_to(value[None], (count,) + value.shape)
    return lax.all_to_all(copies.reshape(-1, value.shape[1]), axes, 0, 0, tiled=True)


def swap(value, axis):
    return lax.ppermute(value, axis, [(0, 1), (1, 0)])


def halves(value, index):
    half = value.shape[0] // 2
    own = lax.dynamic_slice_in_dim(value, index * half, half, 0)
    return own, lax.dynamic_slice_in_dim(value, (1 - index) * half, half, 0)


def in_order(own, other, index, dim):
    return jnp.where(
        index == 0,
        jnp.concatenate([own, other], dim),
        jnp.concatenate([other, own], dim),
    )


def shards(activations, weight, basis):
    core, y_hi, z = (lax.axis_index(name) for name in ("core", "y_hi", "z"))
    partial_value = lax.dot_general(
        activations, basis, (((1,), (1,)), ((), ())), preferred_element_type=jnp.float32
    )
    rank_width = basis.shape[0]
    codes = exchange_gather(exchange_sum(partial_value, CH, 16), CH, 16)

    strip = rank_width // 8
    own_columns = lax.dynamic_slice_in_dim(codes, z * strip, strip, 1)
    other_columns = lax.dynamic_slice_in_dim(codes, y_hi * (rank_width // 2), rank_width // 2, 1)
    gram_part = lax.dot_general(
        own_columns,
        other_columns,
        (((0,), (0,)), ((), ())),
        precision=lax.Precision.HIGHEST,
        preferred_element_type=jnp.float32,
    )
    gram_part = exchange_gather(exchange_sum(gram_part, TOK, 16), TOK, 16)
    gram_rows = in_order(gram_part, swap(gram_part, "y_hi"), y_hi, 1)
    gram = lax.all_gather(gram_rows, "z", axis=0, tiled=True)

    codes_low = codes.astype(jnp.bfloat16)
    local_moments = lax.dot_general(
        activations, codes_low, (((0,), (0,)), ((), ())), preferred_element_type=jnp.float32
    )
    own, other = halves(local_moments, core)
    own = own + swap(other, "core")
    own = exchange_gather(exchange_sum(own, PLANE, 8), PLANE, 8)
    moments = in_order(own, swap(own, "core"), core, 0)

    channels = weight.shape[1]
    rows = weight.shape[0] // 16
    by_z = weight.reshape(2, 8, rows, channels).swapaxes(0, 1).reshape(-1, channels)
    rounded = lax.reduce_precision(moments, 8, 7)
    rest = moments - rounded
    rest_rounded = lax.reduce_precision(rest, 8, 7)
    parts = [rounded, rest_rounded, rest - rest_rounded]
    cross = sum(product(by_z, part.astype(jnp.bfloat16)) for part in parts)
    cross = lax.psum_scatter(cross, "z", scatter_dimension=0, tiled=True)
    own, other = halves(cross, y_hi)
    cross = own + swap(other, "y_hi")

    inverse = damped_inverse(gram)
    return jnp.dot(
        cross, inverse, precision=lax.Precision.HIGHEST, preferred_element_type=jnp.float32
    )


def solution(mesh):
    names = tuple(name for name, _ in AXES)
    fine = Mesh(mesh.devices.reshape([size for _, size in AXES]), names)
    in_specs = (P(TOK, CH), P(TOK, CH), P(None, CH))
    out_specs = P(TOK + CH, None)
    return jax.shard_map(shards, mesh=fine, in_specs=in_specs, out_specs=out_specs, check_vma=False)
```

time: 996 us -> 315 us (0.32)
  waiting for transfers between devices: 598 us -> 102 us
  other arithmetic: 264 us -> 2.39 us
  blocking collectives: 0 us -> 94.5 us
  Pallas kernels: 0 us -> 52.7 us
  matrix products: 58.2 us -> 15.1 us
  local copies, waits for them, and re-layouts: 46.9 us -> 17.6 us
  starting transfers between devices: 0.13 us -> 15.7 us
    psum x2 -> x0, waiting for transfers between devices: 289 us -> none  [the longest x1 152 us: shards(): codes = lax.psum(partial_value, 'ch')]
    another operation x33 -> x0, other arithmetic: 251 us -> none  [the longest x30 168 us: shards(): lower = jnp.linalg.cholesky(damped)]
    unnamed x5 -> x3, waiting for transfers between devices: 209 us -> 13.5 us
    all_to_all x0 -> x5, blocking collectives: none -> 94.5 us  [the longest x3 66.9 us: exchange_sum(): received = lax.all_to_all(value, axes, 0, 0, tiled=True)]
    pallas_call x0 -> x1, Pallas kernels: none -> 52.7 us  [damped_inverse(): pl.pallas_call(inverse_kernel, out_shape=jax.ShapeDtypeStruct((size, size...]
    all_gather x1, waiting for transfers between devices: 99.8 us -> 51.3 us  [shards(): gram = lax.all_gather(gram_rows, 'z', axis=0, tiled=True)]
    another operation x44 -> x0, matrix products: 43 us -> none  [the longest x14 25.9 us: shards(): lower = jnp.linalg.cholesky(damped)]
    another operation x70 -> x0, local copies, waits for them, and re-layouts: 29.1 us -> none
  transfers between devices with their start and end apart: 4 -> 7, of which waited for: 4 -> 6; matrix products, arithmetic and copies ran while one was open for 0% -> 1% of each run, Pallas kernels for 0% -> 17%
where the time goes in v1:
time: 315 us; the launch traced here: 314 us
  waiting for transfers between devices  102 us (32%)
  blocking collectives  94.5 us (30%)
  Pallas kernels  52.7 us (17%)
  local copies, waits for them, and re-layouts  17.6 us (6%)
  starting transfers between devices  15.7 us (5%)
  matrix products  15.1 us (5%)
  between operations  13.6 us (4%)
    all_to_all x3, blocking collectives, exchange_sum(): received = lax.all_to_all(value, axes, 0, 0, tiled=True)  66.9 us
    pallas_call x1, Pallas kernels, damped_inverse(): pl.pallas_call(inverse_kernel, out_shape=jax.ShapeDtypeStruct((size, size...  52.7 us
    all_gather x1, waiting for transfers between devices, shards(): gram = lax.all_gather(gram_rows, 'z', axis=0, tiled=True)  51.3 us
    all_to_all x2, blocking collectives, exchange_gather(): lax.all_to_all(copies.reshape(-1, value.shape[1]), axes, 0, 0, tiled=True)  27.6 us
    all_to_all x1, waiting for transfers between devices, exchange_gather(): lax.all_to_all(copies.reshape(-1, value.shape[1]), axes, 0, 0, tiled=True)  25.7 us
    unnamed x3, waiting for transfers between devices  13.5 us
    unnamed x15, local copies, waits for them, and re-layouts  13 us
    ppermute x4, waiting for transfers between devices, swap(): return lax.ppermute(value, axis, [(0, 1), (1, 0)])  11.6 us
  transfers between devices with their start and end apart: 7, of which 6 were waited for; matrix products, arithmetic and copies ran while one was open for 1% of the time, Pallas kernels for 17%

profile of v1, /device:TPU:1, one launch (start us, length us, event | category | flops | bytes accessed | tf_op | source)
XLA Modules:
  0.0 313.8 jit_solution(4052158936084268287)
XLA Ops:
  6.5 1.2 copy-done
  7.8 1.4 fusion.14
  9.2 38.0 %all_to_all.54 = f32[16,16,1024]{2,1,0:T(8,128)S(1)} all-to-all(f32[16,16,1024]{2,1,0:T(8,128)S(1)} %bitcast.28), channel_id=1, replica_groups=mesh['x'=4,'y_lo'=2,'core'=2,'y_hi'=2,'z'=8] {'y_hi','z'}, dimensions={0} | all-to-all | bytes 2097152 | tf_op jit(solution)/shard_map/all_to_all | solution.py:177
  47.3 1.1 broadcast_in_dim.6
  48.3 6.0 %all-to-all-start.1 = ((f32[16,16,1024]{2,1,0:T(8,128)}), f32[16,16,1024]{2,1,0:T(8,128)S(1)}, u32[]{:S(2)}, u32[]{:S(2)}) async-start(f32[16,16,1024]{2,1,0:T(8,128)} %broadcast_in_dim.6), calls=%async_computation.1 | async-start | bytes 2097152 | tf_op jit(solution)/shard_map/all_to_all | solution.py:183
  54.4 25.7 %all-to-all-done.1 = f32[16,16,1024]{2,1,0:T(8,128)S(1)} async-done(((f32[16,16,1024]{2,1,0:T(8,128)}), f32[16,16,1024]{2,1,0:T(8,128)S(1)}, u32[]{:S(2)}, u32[]{:S(2)}) %all-to-all-start.1) | async-done | bytes 1048608 | tf_op jit(solution)/shard_map/all_to_all | solution.py:183
  80.1 1.1 copy-done.3
  81.2 1.7 fusion.7
  82.9 1.0 dynamic-slice_bitcast_fusion
  83.9 2.9 collective-permute-start
  86.9 2.6 collective-permute-done
  89.5 1.4 bitcast_add_fusion
  90.9 18.2 %all_to_all.55 = f32[8,32,1024]{2,1,0:T(8,128)S(1)} all-to-all(f32[8,32,1024]{2,1,0:T(8,128)S(1)} %bitcast.27), channel_id=1, replica_groups=mesh['x'=4,'y_lo'=2,'core'=2,'y_hi'=2,'z'=8] {'x','y_lo'}, dimensions={0} | all-to-all | bytes 2097152 | tf_op jit(solution)/shard_map/all_to_all | solution.py:177
  109.2 17.1 %all_to_all.56 = f32[8,32,1024]{2,1,0:T(8,128)S(1)} all-to-all(f32[8,32,1024]{2,1,0:T(8,128)S(1)} %broadcast_in_dim.7), channel_id=1, replica_groups=mesh['x'=4,'y_lo'=2,'core'=2,'y_hi'=2,'z'=8] {'x','y_lo'}, dimensions={0} | all-to-all | bytes 2097152 | tf_op jit(solution)/shard_map/all_to_all | solution.py:183
  126.3 2.7 collective-permute-start.1
  129.0 1.3 copy.5
  131.3 1.4 fusion.3
  132.7 1.4 fusion.2
  134.0 3.3 %add_bitcast_fusion = f32[896,1024]{0,1:T(8,128)} fusion(f32[1024,896]{1,0:T(8,128)S(1)} %fusion.2, f32[1024,896]{1,0:T(8,128)S(1)} %fusion.3, bf16[896,512]{1,0:T(8,128)(2,1)S(1)} %bitcast.35, f32[256,1024]{1,0:T(8,128)S(1)} %collective-permute-done.1, f32[256,1024]{1,0:T(8,128)S(1)} %bitcast.32, pred[]{:T(512)S(6)} %eq.6), kind=kOutput, calls=%fused_computation | convolution fusion | flops 945553408 | bytes 14024705 | tf_op jit(solution)/shard_map/dot_general | solution.py:97
  137.3 5.1 %copy.6 = f32[896,1024]{1,0:T(8,128)} copy(f32[896,1024]{0,1:T(8,128)} %add_bitcast_fusion) | data formatting | bytes 7340032
  142.5 1.1 copy-done.4
  144.1 10.7 %all_to_all.57 = f32[16,8,512]{2,1,0:T(8,128)S(1)} all-to-all(f32[16,8,512]{2,1,0:T(8,128)S(1)} %convolution_bitcast_fusion), channel_id=1, replica_groups=mesh['x'=4,'y_lo'=2,'core'=2,'y_hi'=2,'z'=8] {'x','y_lo','core'}, dimensions={0} | all-to-all | bytes 524288 | tf_op jit(solution)/shard_map/all_to_all | solution.py:177
  154.8 10.5 %all_to_all.58 = f32[16,8,512]{2,1,0:T(8,128)S(1)} all-to-all(f32[16,8,512]{2,1,0:T(8,128)S(1)} %broadcast_in_dim.8), channel_id=1, replica_groups=mesh['x'=4,'y_lo'=2,'core'=2,'y_hi'=2,'z'=8] {'x','y_lo','core'}, dimensions={0} | all-to-all | bytes 524288 | tf_op jit(solution)/shard_map/all_to_all | solution.py:183
  166.3 8.0 %collective-permute-done.3 = f32[128,512]{1,0:T(8,128)S(1)} collective-permute-done((f32[128,512]{1,0:T(8,128)S(1)}, f32[128,512]{1,0:T(8,128)S(1)}, u32[]{:S(2)}, u32[]{:S(2)}) %collective-permute-start.3) | collective-permute-done | bytes 262176 | tf_op jit(solution)/shard_map/ppermute | solution.py:187
  175.2 13.5 %reduce-scatter.4.cloned.1.call-done = f32[112,1024]{1,0:T(8,128)} async-done(((f32[896,1024]{1,0:T(8,128)}), f32[112,1024]{1,0:T(8,128)}) %reduce-scatter.4.cloned.1.call-update) | async-done | bytes 458768
  188.7 1.1 constant_dynamic-slice_fusion
  190.0 3.0 collective-permute-start.2
  193.0 51.3 %all-gather.2.cloned.1.call-done.gram_ref = f32[1024,1024]{1,0:T(8,128)} async-done(((f32[128,1024]{1,0:T(8,128)}), f32[1024,1024]{1,0:T(8,128)}) %all-gather.2.cloned.1.call-update) | async-done | bytes 4194320 | tf_op jit(solution)/shard_map/all_gather | solution.py:224
  244.3 2.2 copy-done.2
  246.5 52.7 %shard_map.37 = f32[1024,1024]{1,0:T(8,128)S(1)} custom-call(f32[1024,1024]{1,0:T(8,128)S(1)} %copy-done.2), custom_call_target="tpu_custom_call" | custom-call | flops 12884901888 | bytes 8388608 | tf_op jit(solution)/shard_map/pallas_call | solution.py:161
  299.3 1.9 copy-done.1
  301.4 5.6 %fusion.5 = f32[56,1024]{1,0:T(8,128)} fusion(f32[1024,1024]{1,0:T(8,128)} %copy-done.1, f32[56,1024]{0,1:T(8,128)S(1)} %copy.8, f32[56,1024]{0,1:T(8,128)S(1)} %collective-permute-done.2), kind=kOutput, calls=%fused_computation.14 | convolution fusion | flops 704700416 | bytes 4882432 | tf_op jit(solution)/shard_map/dot_general | solution.py:248
  (23 shorter events, 4.1 us)
Async XLA Ops:
  6.5 1.2 copy-start
  47.2 34.0 %copy-start.5 = (bf16[256,512]{1,0:T(8,128)(2,1)S(1)}, bf16[256,512]{1,0:T(8,128)(2,1)}, u32[]{:S(2)}) copy-start(bf16[256,512]{1,0:T(8,128)(2,1)} %param.3) | copy-start | bytes 786436
  48.3 31.8 %all-to-all-start.1 = ((f32[16,16,1024]{2,1,0:T(8,128)}), f32[16,16,1024]{2,1,0:T(8,128)S(1)}, u32[]{:S(2)}, u32[]{:S(2)}) async-start(f32[16,16,1024]{2,1,0:T(8,128)} %broadcast_in_dim.6), calls=%async_computation.1 | async-start | bytes 2097152 | tf_op jit(solution)/shard_map/all_to_all | solution.py:183
  54.3 134.4 %reduce-scatter.4.cloned.1.call-start = ((), (), s32[]{:S(2)}) async-start(), calls=%async_computation.8 | async-start | bytes 4128768
  80.1 1.1 copy-start.3
  83.9 5.6 %collective-permute-start = (f32[256,1024]{1,0:T(8,128)}, f32[256,1024]{1,0:T(8,128)}, u32[]{:S(2)}, u32[]{:S(2)}) collective-permute-start(f32[256,1024]{1,0:T(8,128)} %dynamic-slice_bitcast_fusion), channel_id=1, source_target_pairs={{0,16},{16,0},{1,17},{17,1},{2,18},{18,2},{3,19},{19,3},{4,20},{20... | collective-permute-start | bytes 3145736 | tf_op jit(solution)/shard_map/ppermute | solution.py:187
  126.3 5.0 %collective-permute-start.1 = (f32[256,1024]{1,0:T(8,128)S(1)}, f32[256,1024]{1,0:T(8,128)S(1)}, u32[]{:S(2)}, u32[]{:S(2)}) collective-permute-start(f32[256,1024]{1,0:T(8,128)S(1)} %bitcast.29), channel_id=1, source_target_pairs={{0,16},{16,0},{1,17},{17,1},{2,18},{18,2},{3,19},{19,3},{4,20},{20... | collective-permute-start | bytes 3145736 | tf_op jit(solution)/shard_map/ppermute | solution.py:187
  142.4 1.2 copy-start.4
  142.4 101.9 %all-gather.2.cloned.1.call-start = ((), (), s32[]{:S(2)}) async-start(), calls=%async_computation.7 | async-start | bytes 4718592 | tf_op jit(solution)/shard_map/all_gather | solution.py:224
  165.3 9.0 %collective-permute-start.3 = (f32[128,512]{1,0:T(8,128)S(1)}, f32[128,512]{1,0:T(8,128)S(1)}, u32[]{:S(2)}, u32[]{:S(2)}) collective-permute-start(f32[128,512]{1,0:T(8,128)S(1)} %bitcast.36), channel_id=1, source_target_pairs={{0,8},{8,0},{1,9},{9,1},{2,10},{10,2},{3,11},{11,3},{4,12},{12,4},... | collective-permute-start | bytes 786440 | tf_op jit(solution)/shard_map/ppermute | solution.py:187
  190.0 111.4 %collective-permute-start.2 = (f32[56,1024]{0,1:T(8,128)S(1)}, f32[56,1024]{0,1:T(8,128)S(1)}, u32[]{:S(2)}, u32[]{:S(2)}) collective-permute-start(f32[56,1024]{0,1:T(8,128)S(1)} %copy.9), channel_id=1, source_target_pairs={{0,8},{8,0},{1,9},{9,1},{2,10},{10,2},{3,11},{11,3},{4,12},{12,4},... | collective-permute-start | bytes 688136 | tf_op jit(solution)/shard_map/ppermute | solution.py:187
  244.3 2.2 copy-start.2
  299.3 1.9 copy-start.1
Sparse Core Ops, SparseCore 0:
  142.5 46.1 reduce-scatter.3
  190.5 53.7 all-gather.1

commit v2 on v1

--- a/solution.py
+++ b/solution.py
@@ -9,6 +9,7 @@
 damping = 0.1
 
 SUB, LANE = 8, 128
+STRIP = 5
 AXES = (("x", 4), ("y_lo", 2), ("core", 2), ("y_hi", 2), ("z", 8))
 TOK = ("x", "y_lo", "core")
 PLANE = ("x", "y_lo")
@@ -98,7 +99,7 @@
 
 
 def inverse_kernel(gram_ref, out_ref, left_ref, right_ref, block_ref):
-    size = gram_ref.shape[0]
+    size = out_ref.shape[0]
     blocks = size // LANE
     tile = 256
     row = lax.broadcasted_iota(jnp.int32, (LANE, LANE), 0)
@@ -106,13 +107,18 @@
     diagonal = row == column
     total = jnp.zeros((LANE, LANE), jnp.float32)
     for b in range(blocks):
-        own = slice(b * LANE, (b + 1) * LANE)
-        total = total + jnp.where(diagonal, gram_ref[own, own], 0.0)
+        total = total + jnp.where(diagonal, gram_ref[b * LANE : (b + 1) * LANE, 0:LANE], 0.0)
     ridge = damping * jnp.sum(total) / size
-    out_ref[...] = gram_ref[...]
-    for b in range(blocks):
-        own = slice(b * LANE, (b + 1) * LANE)
-        out_ref[own, own] = gram_ref[own, own] + jnp.where(diagonal, ridge, 0.0)
+    for a in range(blocks):
+        for d in range(STRIP):
+            b = (a + d) % blocks
+            ours, theirs = slice(a * LANE, (a + 1) * LANE), slice(b * LANE, (b + 1) * LANE)
+            block = gram_ref[ours, d * LANE : (d + 1) * LANE]
+            if d == 0:
+                block = block + jnp.where(diagonal, ridge, 0.0)
+            out_ref[ours, theirs] = block
+            if 0 < d < blocks // 2:
+                out_ref[theirs, ours] = block.T
 
     def keep(rows):
         for r in range(LANE // SUB):
@@ -173,6 +179,40 @@
     )(gram)
 
 
+def cross_kernel(core_ref, weight_ref, own_ref, other_ref, out_ref):
+    width = own_ref.shape[0]
+    rows = weight_ref.shape[0] // 16
+    tile = 256
+    core = core_ref[0]
+    left = [
+        weight_ref[:, pl.ds(pl.multiple_of(start * width, width), width)]
+        for start in (core, 1 - core)
+    ]
+    left = jnp.concatenate(left, 1)
+    for n in range(out_ref.shape[1] // tile):
+        columns = slice(n * tile, (n + 1) * tile)
+        parts = zip(split(own_ref[:, columns]), split(other_ref[:, columns]))
+        result = tree_sum([product(left, jnp.concatenate(pair, 0)) for pair in parts])
+        for y in range(2):
+            for z in range(8):
+                source, target = (y * 8 + z) * rows, (z * 2 + y) * rows
+                out_ref[target : target + rows, columns] = result[source : source + rows, :]
+
+
+def cross_terms(core, weight, own, other):
+    whole = pl.BlockSpec(memory_space=pltpu.VMEM)
+    return pl.pallas_call(
+        cross_kernel,
+        out_shape=jax.ShapeDtypeStruct((weight.shape[0], own.shape[1]), jnp.float32),
+        in_specs=[pl.BlockSpec(memory_space=pltpu.SMEM), whole, whole, whole],
+        out_specs=whole,
+        compiler_params=pltpu.CompilerParams(vmem_limit_bytes=40 * 2**20),
+        cost_estimate=pl.CostEstimate(
+            flops=6 * weight.size * own.shape[1], bytes_accessed=8 * 2**20, transcendentals=0
+        ),
+    )(core.astype(jnp.int32)[None], weight, own, other)
+
+
 def exchange_sum(value, axes, count):
     received = lax.all_to_all(value, axes, 0, 0, tiled=True)
     return received.reshape(count, -1, value.shape[1]).sum(0)
@@ -193,14 +233,6 @@
     return own, lax.dynamic_slice_in_dim(value, (1 - index) * half, half, 0)
 
 
-def in_order(own, other, index, dim):
-    return jnp.where(
-        index == 0,
-        jnp.concatenate([own, other], dim),
-        jnp.concatenate([other, own], dim),
-    )
-
-
 def shards(activations, weight, basis):
     core, y_hi, z = (lax.axis_index(name) for name in ("core", "y_hi", "z"))
     partial_value = lax.dot_general(
@@ -209,19 +241,16 @@
     rank_width = basis.shape[0]
     codes = exchange_gather(exchange_sum(partial_value, CH, 16), CH, 16)
 
-    strip = rank_width // 8
-    own_columns = lax.dynamic_slice_in_dim(codes, z * strip, strip, 1)
-    other_columns = lax.dynamic_slice_in_dim(codes, y_hi * (rank_width // 2), rank_width // 2, 1)
+    wide = jnp.concatenate([codes, codes[:, : (STRIP - 1) * LANE]], 1)
+    own_columns = lax.dynamic_slice_in_dim(wide, z * LANE, STRIP * LANE, 1)
     gram_part = lax.dot_general(
+        own_columns[:, :LANE],
         own_columns,
-        other_columns,
         (((0,), (0,)), ((), ())),
         precision=lax.Precision.HIGHEST,
         preferred_element_type=jnp.float32,
     )
-    gram_part = exchange_gather(exchange_sum(gram_part, TOK, 16), TOK, 16)
-    gram_rows = in_order(gram_part, swap(gram_part, "y_hi"), y_hi, 1)
-    gram = lax.all_gather(gram_rows, "z", axis=0, tiled=True)
+    gram_sum = exchange_sum(gram_part, TOK, 16)
 
     codes_low = codes.astype(jnp.bfloat16)
     local_moments = lax.dot_general(
@@ -229,22 +258,17 @@
     )
     own, other = halves(local_moments, core)
     own = own + swap(other, "core")
+    gram_rows = exchange_gather(gram_sum, TOK, 16)
+    own, gram_rows = lax.optimization_barrier((own, gram_rows))
+    gram = lax.all_gather(gram_rows, "z", axis=0, tiled=True)
     own = exchange_gather(exchange_sum(own, PLANE, 8), PLANE, 8)
-    moments = in_order(own, swap(own, "core"), core, 0)
-
-    channels = weight.shape[1]
-    rows = weight.shape[0] // 16
-    by_z = weight.reshape(2, 8, rows, channels).swapaxes(0, 1).reshape(-1, channels)
-    rounded = lax.reduce_precision(moments, 8, 7)
-    rest = moments - rounded
-    rest_rounded = lax.reduce_precision(rest, 8, 7)
-    parts = [rounded, rest_rounded, rest - rest_rounded]
-    cross = sum(product(by_z, part.astype(jnp.bfloat16)) for part in parts)
+    cross = cross_terms(core, weight, own, swap(own, "core"))
+    cross, gram = lax.optimization_barrier((cross, gram))
     cross = lax.psum_scatter(cross, "z", scatter_dimension=0, tiled=True)
+    inverse = damped_inverse(gram)
+    cross, inverse = lax.optimization_barrier((cross, inverse))
     own, other = halves(cross, y_hi)
     cross = own + swap(other, "y_hi")
-
-    inverse = damped_inverse(gram)
     return jnp.dot(
         cross, inverse, precision=lax.Precision.HIGHEST, preferred_element_type=jnp.float32
     )

time: 315 us -> 240 us (0.76)
  waiting for transfers between devices: 102 us -> 40.7 us
  blocking collectives: 94.5 us -> 85.4 us
  matrix products: 15.1 us -> 8.07 us
  Pallas kernels: 52.7 us -> 56.2 us
    all_gather x1, waiting for transfers between devices: 51.3 us -> 0.01 us  [shards(): gram = lax.all_gather(gram_rows, 'z', axis=0, tiled=True)]
    unnamed x3 -> x2, waiting for transfers between devices: 13.5 us -> 0.03 us
    all_to_all x2 -> x1, blocking collectives: 27.6 us -> 17.1 us  [exchange_gather(): lax.all_to_all(copies.reshape(-1, value.shape[1]), axes, 0, 0, tiled=True)]
    dot_general x4 -> x1, matrix products: 6.47 us -> 0.55 us  [shards(): lax.dot_general(own_columns[:, :LANE], own_columns, (((0,), (0,)), ((), (...]
    all_to_all x1 -> x2, waiting for transfers between devices: 25.7 us -> 31.3 us  [exchange_gather(): lax.all_to_all(copies.reshape(-1, value.shape[1]), axes, 0, 0, tiled=True)]
    unnamed x15 -> x18, local copies, waits for them, and re-layouts: 13 us -> 8.79 us
    all_to_all x1 -> x2, starting transfers between devices: 5.98 us -> 9.81 us  [exchange_gather(): lax.all_to_all(copies.reshape(-1, value.shape[1]), axes, 0, 0, tiled=True)]
    ppermute x4 -> x3, starting transfers between devices: 9.59 us -> 7 us  [swap(): return lax.ppermute(value, axis, [(0, 1), (1, 0)])]
  transfers between devices with their start and end apart: 7 -> 7, of which waited for: 6 -> 4; matrix products, arithmetic and copies ran while one was open for 1% -> 3% of each run, Pallas kernels for 17% -> 24%
where the time goes in v2:
time: 240 us; the launch traced here: 239 us
  blocking collectives  85.4 us (36%)
  Pallas kernels  56.2 us (23%)
  waiting for transfers between devices  40.7 us (17%)
  starting transfers between devices  16.9 us (7%)
  local copies, waits for them, and re-layouts  15.4 us (6%)
  between operations  13.6 us (6%)
  matrix products  8.07 us (3%)
  other arithmetic  2.78 us (1%)
    all_to_all x3, blocking collectives, exchange_sum(): received = lax.all_to_all(value, axes, 0, 0, tiled=True)  68.3 us
    pallas_call x1, Pallas kernels, damped_inverse(): pl.pallas_call(inverse_kernel, out_shape=jax.ShapeDtypeStruct((size, size...  53.1 us
    all_to_all x2, waiting for transfers between devices, exchange_gather(): lax.all_to_all(copies.reshape(-1, value.shape[1]), axes, 0, 0, tiled=True)  31.3 us
    all_to_all x1, blocking collectives, exchange_gather(): lax.all_to_all(copies.reshape(-1, value.shape[1]), axes, 0, 0, tiled=True)  17.1 us
    all_to_all x2, starting transfers between devices, exchange_gather(): lax.all_to_all(copies.reshape(-1, value.shape[1]), axes, 0, 0, tiled=True)  9.81 us
    ppermute x3, waiting for transfers between devices, swap(): return lax.ppermute(value, axis, [(0, 1), (1, 0)])  9.38 us
    unnamed x18, local copies, waits for them, and re-layouts  8.79 us
    ppermute x3, starting transfers between devices, swap(): return lax.ppermute(value, axis, [(0, 1), (1, 0)])  7 us
  transfers between devices with their start and end apart: 7, of which 4 were waited for; matrix products, arithmetic and copies ran while one was open for 3% of the time, Pallas kernels for 24%

profile of v2, /device:TPU:1, one launch (start us, length us, event | category | flops | bytes accessed | tf_op | source)
XLA Modules:
  0.0 239.1 jit_solution(18373759347417336458)
XLA Ops:
  6.5 1.2 copy-done
  7.8 1.4 fusion.8
  9.2 38.0 %all_to_all.53 = f32[16,16,1024]{2,1,0:T(8,128)S(1)} all-to-all(f32[16,16,1024]{2,1,0:T(8,128)S(1)} %bitcast.23), channel_id=1, replica_groups=mesh['x'=4,'y_lo'=2,'core'=2,'y_hi'=2,'z'=8] {'y_hi','z'}, dimensions={0} | all-to-all | bytes 2097152 | tf_op jit(solution)/shard_map/all_to_all | solution.py:217
  47.3 1.1 broadcast_in_dim.9
  48.4 6.0 %all-to-all-start.1 = ((f32[16,16,1024]{2,1,0:T(8,128)}), f32[16,16,1024]{2,1,0:T(8,128)S(1)}, u32[]{:S(2)}, u32[]{:S(2)}) async-start(f32[16,16,1024]{2,1,0:T(8,128)} %broadcast_in_dim.9), calls=%async_computation.1 | async-start | bytes 2097152 | tf_op jit(solution)/shard_map/all_to_all | solution.py:223
  54.3 25.8 %all-to-all-done.1 = f32[16,16,1024]{2,1,0:T(8,128)S(1)} async-done(((f32[16,16,1024]{2,1,0:T(8,128)}), f32[16,16,1024]{2,1,0:T(8,128)S(1)}, u32[]{:S(2)}, u32[]{:S(2)}) %all-to-all-start.1) | async-done | bytes 1048608 | tf_op jit(solution)/shard_map/all_to_all | solution.py:223
  80.1 0.5 fusion.1
  80.6 1.3 copy-done.5
  81.9 1.1 dynamic-slice_bitcast_fusion
  83.0 2.9 %collective-permute-start = (f32[256,1024]{0,1:T(8,128)}, f32[256,1024]{0,1:T(8,128)}, u32[]{:S(2)}, u32[]{:S(2)}) collective-permute-start(f32[256,1024]{0,1:T(8,128)} %dynamic-slice_bitcast_fusion), channel_id=1, source_target_pairs={{0,16},{16,0},{1,17},{17,1},{2,18},{18,2},{3,19},{19,3},{4,20},{20... | collective-permute-start | bytes 3145736 | tf_op jit(solution)/shard_map/ppermute | solution.py:227
  86.0 0.2 fusion
  86.2 0.5 convolution_bitcast_fusion
  86.7 12.5 %all_to_all.54 = f32[16,8,640]{2,1,0:T(8,128)S(1)} all-to-all(f32[16,8,640]{2,1,0:T(8,128)S(1)} %convolution_bitcast_fusion), channel_id=1, replica_groups=mesh['x'=4,'y_lo'=2,'core'=2,'y_hi'=2,'z'=8] {'x','y_lo','core'}, dimensions={0} | all-to-all | bytes 655360 | tf_op jit(solution)/shard_map/all_to_all | solution.py:217
  99.2 0.8 broadcast_in_dim.10
  100.0 3.8 %all-to-all-start.3 = ((f32[16,8,640]{2,1,0:T(8,128)}), f32[16,8,640]{2,1,0:T(8,128)S(1)}, u32[]{:S(2)}, u32[]{:S(2)}) async-start(f32[16,8,640]{2,1,0:T(8,128)} %broadcast_in_dim.10), calls=%async_computation.3 | async-start | bytes 655360 | tf_op jit(solution)/shard_map/all_to_all | solution.py:223
  103.9 2.5 %bitcast_add_fusion = f32[256,1024]{0,1:T(8,128)} fusion(f32[256,1024]{0,1:T(8,128)} %collective-permute-done, f32[1024,512]{1,0:T(8,128)S(1)} %copy-done.6, s32[]{:T(128)S(6)} %select_n.15), kind=kLoop, calls=%fused_computation.3 | loop fusion | flops 262144 | bytes 3145732 | tf_op jit(solution)/shard_map/add | solution.py:260
  106.4 5.5 %all-to-all-done.3 = f32[16,8,640]{2,1,0:T(8,128)S(1)} async-done(((f32[16,8,640]{2,1,0:T(8,128)}), f32[16,8,640]{2,1,0:T(8,128)S(1)}, u32[]{:S(2)}, u32[]{:S(2)}) %all-to-all-start.3) | async-done | bytes 327712 | tf_op jit(solution)/shard_map/all_to_all | solution.py:223
  111.9 0.7 copy-done.7
  112.7 2.6 %copy.4 = f32[256,1024]{1,0:T(8,128)} copy(f32[256,1024]{0,1:T(8,128)} %bitcast_add_fusion) | data formatting | bytes 2097152 | tf_op jit(solution)/shard_map/optimization_barrier | solution.py:262
  115.3 17.8 %all_to_all.55 = f32[8,32,1024]{2,1,0:T(8,128)S(1)} all-to-all(f32[8,32,1024]{2,1,0:T(8,128)} %bitcast.22), channel_id=1, replica_groups=mesh['x'=4,'y_lo'=2,'core'=2,'y_hi'=2,'z'=8] {'x','y_lo'}, dimensions={0} | all-to-all | bytes 2097152 | tf_op jit(solution)/shard_map/all_to_all | solution.py:217
  133.3 17.1 %all_to_all.56 = f32[8,32,1024]{2,1,0:T(8,128)S(1)} all-to-all(f32[8,32,1024]{2,1,0:T(8,128)S(1)} %broadcast_in_dim.11), channel_id=1, replica_groups=mesh['x'=4,'y_lo'=2,'core'=2,'y_hi'=2,'z'=8] {'x','y_lo'}, dimensions={0} | all-to-all | bytes 2097152 | tf_op jit(solution)/shard_map/all_to_all | solution.py:223
  150.4 2.7 %collective-permute-start.1 = (f32[256,1024]{1,0:T(8,128)S(1)}, f32[256,1024]{1,0:T(8,128)S(1)}, u32[]{:S(2)}, u32[]{:S(2)}) collective-permute-start(f32[256,1024]{1,0:T(8,128)S(1)} %bitcast.17), channel_id=1, source_target_pairs={{0,16},{16,0},{1,17},{17,1},{2,18},{18,2},{3,19},{19,3},{4,20},{20... | collective-permute-start | bytes 3145736 | tf_op jit(solution)/shard_map/ppermute | solution.py:227
  153.2 2.3 collective-permute-done.1.other_ref
  155.4 3.1 %shard_map.37 = f32[896,1024]{1,0:T(8,128)S(1)} custom-call(s32[1]{0:T(128)} %bitcast.core_ref, bf16[896,512]{1,0:T(8,128)(2,1)S(1)} %copy-done.4, f32[256,1024]{1,0:T(8,128)S(1)} %bitcast.18, f32[256,1024]{1,0:T(8,128)S(1)} %collective-permute-done.1.other_ref), custom_call_target="tpu_custom_call" | custom-call | flops 2818572288 | bytes 8388608 | tf_op jit(solution)/shard_map/pallas_call | solution.py:204
  158.6 1.8 copy-done.2
  160.4 1.7 copy-done.3
  162.1 53.1 %shard_map.38 = f32[1024,1024]{1,0:T(8,128)S(1)} custom-call(f32[1024,640]{1,0:T(8,128)S(1)} %copy-done.3), custom_call_target="tpu_custom_call" | custom-call | flops 12884901888 | bytes 8388608 | tf_op jit(solution)/shard_map/pallas_call | solution.py:167
  215.2 1.9 copy-done.1
  217.2 1.0 constant_dynamic-slice_fusion
  218.1 1.3 collective-permute-start.2
  219.5 7.1 %collective-permute-done.2 = f32[56,1024]{1,0:T(8,128)S(1)} collective-permute-done((f32[56,1024]{1,0:T(8,128)S(1)}, f32[56,1024]{1,0:T(8,128)S(1)}, u32[]{:S(2)}, u32[]{:S(2)}) %collective-permute-start.2) | collective-permute-done | bytes 229408 | tf_op jit(solution)/shard_map/ppermute | solution.py:227
  226.6 5.6 %fusion.3 = f32[56,1024]{1,0:T(8,128)} fusion(f32[1024,1024]{1,0:T(8,128)} %copy-done.1, f32[56,1024]{1,0:T(8,128)S(1)} %collective-permute-done.2, f32[112,1024]{1,0:T(8,128)} %reduce-scatter.2.cloned.1.call-done, s32[]{:T(128)S(6)} %select_n.18), kind=kOutput, calls=%fused_computation.8 | convolution fusion | flops 704700416 | bytes 4882436 | tf_op jit(solution)/shard_map/dot_general | solution.py:272
  (24 shorter events, 0.4 us)
Async XLA Ops:
  6.5 1.2 copy-start
  47.2 32.9 %copy-start.8 = (bf16[256,512]{1,0:T(8,128)(2,1)S(1)}, bf16[256,512]{1,0:T(8,128)(2,1)}, u32[]{:S(2)}) copy-start(bf16[256,512]{1,0:T(8,128)(2,1)} %param.3) | copy-start | bytes 786436
  48.4 31.8 %all-to-all-start.1 = ((f32[16,16,1024]{2,1,0:T(8,128)}), f32[16,16,1024]{2,1,0:T(8,128)S(1)}, u32[]{:S(2)}, u32[]{:S(2)}) async-start(f32[16,16,1024]{2,1,0:T(8,128)} %broadcast_in_dim.9), calls=%async_computation.1 | async-start | bytes 2097152 | tf_op jit(solution)/shard_map/all_to_all | solution.py:223
  80.6 1.3 copy-start.5
  83.0 20.9 %collective-permute-start = (f32[256,1024]{0,1:T(8,128)}, f32[256,1024]{0,1:T(8,128)}, u32[]{:S(2)}, u32[]{:S(2)}) collective-permute-start(f32[256,1024]{0,1:T(8,128)} %dynamic-slice_bitcast_fusion), channel_id=1, source_target_pairs={{0,16},{16,0},{1,17},{17,1},{2,18},{18,2},{3,19},{19,3},{4,20},{20... | collective-permute-start | bytes 3145736 | tf_op jit(solution)/shard_map/ppermute | solution.py:227
  86.2 17.7 %copy-start.6 = (f32[1024,512]{1,0:T(8,128)S(1)}, f32[1024,512]{1,0:T(8,128)}, u32[]{:S(2)}) copy-start(f32[1024,512]{1,0:T(8,128)} %copy-done.5) | copy-start | bytes 6291460
  100.0 11.9 %all-to-all-start.3 = ((f32[16,8,640]{2,1,0:T(8,128)}), f32[16,8,640]{2,1,0:T(8,128)S(1)}, u32[]{:S(2)}, u32[]{:S(2)}) async-start(f32[16,8,640]{2,1,0:T(8,128)} %broadcast_in_dim.10), calls=%async_computation.3 | async-start | bytes 655360 | tf_op jit(solution)/shard_map/all_to_all | solution.py:223
  103.8 56.5 %all-gather.2.cloned.1.call-start = ((), (), s32[]{:S(2)}) async-start(), calls=%async_computation.7 | async-start | bytes 2949120 | tf_op jit(solution)/shard_map/all_gather | solution.py:263
  111.9 0.7 copy-start.7
  112.7 104.5 %reduce-scatter.2.cloned.1.call-start = ((), (), s32[]{:S(2)}) async-start(), calls=%async_computation.8 | async-start | bytes 4128768 | tf_op jit(solution)/shard_map/reduce_scatter | solution.py:267
  133.1 22.3 %copy-start.4 = (bf16[896,512]{1,0:T(8,128)(2,1)S(1)}, bf16[896,512]{1,0:T(8,128)(2,1)}, u32[]{:S(2)}) copy-start(bf16[896,512]{1,0:T(8,128)(2,1)} %weight_ref.1) | copy-start | bytes 2752516
  150.4 5.0 %collective-permute-start.1 = (f32[256,1024]{1,0:T(8,128)S(1)}, f32[256,1024]{1,0:T(8,128)S(1)}, u32[]{:S(2)}, u32[]{:S(2)}) collective-permute-start(f32[256,1024]{1,0:T(8,128)S(1)} %bitcast.17), channel_id=1, source_target_pairs={{0,16},{16,0},{1,17},{17,1},{2,18},{18,2},{3,19},{19,3},{4,20},{20... | collective-permute-start | bytes 3145736 | tf_op jit(solution)/shard_map/ppermute | solution.py:227
  158.5 1.8 copy-start.2
  160.4 1.7 copy-start.3
  215.2 2.0 copy-start.1
  218.1 8.4 %collective-permute-start.2 = (f32[56,1024]{1,0:T(8,128)S(1)}, f32[56,1024]{1,0:T(8,128)S(1)}, u32[]{:S(2)}, u32[]{:S(2)}) collective-permute-start(f32[56,1024]{1,0:T(8,128)S(1)} %constant_dynamic-slice_fusion), channel_id=1, source_target_pairs={{0,8},{8,0},{1,9},{9,1},{2,10},{10,2},{3,11},{11,3},{4,12},{12,4},... | collective-permute-start | bytes 688136 | tf_op jit(solution)/shard_map/ppermute | solution.py:227
Sparse Core Ops, SparseCore 0:
  112.8 34.9 all-gather.1
  160.5 46.1 reduce-scatter.1

commit v3 on v2

v3 whole, which is shorter than its diff:
```python
import functools

import jax
import jax.numpy as jnp
from jax import lax
from jax.experimental import pallas as pl
from jax.experimental.pallas import tpu as pltpu
from jax.sharding import Mesh
from jax.sharding import PartitionSpec as P

damping = 0.1

SUB, LANE = 8, 128
NEAR = 1
STRIP = 5
AXES = (("x", 4), ("y_lo", 2), ("core", 2), ("y_hi", 2), ("z", 8))
TOK = ("x", "y_lo", "core")
PLANE = ("x", "y_lo")
CH = ("y_hi", "z")


def tree_sum(terms):
    while len(terms) > 1:
        paired = [a + b for a, b in zip(terms[::2], terms[1::2])]
        terms = paired + ([terms[-1]] if len(terms) % 2 else [])
    return terms[0]


def spread(value):
    return jnp.broadcast_to(value, (SUB, LANE))


def invert_small(entry):
    for k in range(SUB):
        inverse = 1.0 / entry[k, k]
        row = [entry[min(k, j), max(k, j)] for j in range(SUB)]
        scaled = [value * inverse for value in row]
        for i in range(SUB):
            for j in range(i, SUB):
                if i != k and j != k:
                    entry[i, j] = entry[i, j] - scaled[i] * row[j]
        for j in range(SUB):
            if j != k:
                entry[min(k, j), max(k, j)] = scaled[j]
        entry[k, k] = -inverse
    return {place: -value for place, value in entry.items()}


def eliminate(near, pivot):
    return tree_sum([near[j] * spread(pivot[j : j + 1, :]) for j in range(SUB)])


def invert_block(block, between=None):
    sub = lax.broadcasted_iota(jnp.int32, (SUB, LANE), 0)
    lane = lax.broadcasted_iota(jnp.int32, (SUB, LANE), 1)
    panels = LANE // SUB
    rows = [block[r * SUB : (r + 1) * SUB, :] for r in range(panels)]
    for p in range(panels):
        base = p * SUB
        panel = rows[p]
        inside = (lane >= base) & (lane < base + SUB)

        def columns_of(r):
            return [spread(rows[r][:, base + j : base + j + 1]) for j in range(SUB)]

        columns = columns_of(p)
        near = {r: columns_of(r) for r in range(p + 1, min(p + 1 + NEAR, panels))}
        small = invert_small(
            {(i, j): spread(columns[j][i : i + 1, :]) for j in range(SUB) for i in range(j + 1)}
        )
        small_columns = []
        for j in range(SUB):
            column = small[0, j]
            for i in range(1, SUB):
                column = jnp.where(sub == i, small[min(i, j), max(i, j)], column)
            small_columns.append(column)
        wide = jnp.where(inside, jnp.where(lane - base == sub, 1.0, 0.0), panel)
        pivot = eliminate(small_columns, wide)
        left = jnp.concatenate(left_list(jnp.where(lane < base, -panel, panel)), 0)
        right = jnp.concatenate(right_list(pivot), 0)
        change = lax.dot_general(
            left.astype(jnp.bfloat16),
            right.astype(jnp.bfloat16),
            (((0,), (0,)), ((), ())),
            preferred_element_type=jnp.float32,
        )
        for r in range(panels):
            if r in near:
                rows[r] = jnp.where(inside, 0.0, rows[r]) - eliminate(near[r], pivot)
            elif r != p:
                rows[r] = jnp.where(inside, 0.0, rows[r]) - change[r * SUB : (r + 1) * SUB, :]
        rows[p] = pivot
        if between is not None:
            between(p)
    return rows


def split(value):
    high = value.astype(jnp.bfloat16).astype(jnp.float32)
    rest = value - high
    middle = rest.astype(jnp.bfloat16).astype(jnp.float32)
    return high, middle, rest - middle


def left_list(value):
    high, middle, low = split(value)
    return [high, middle, high, middle, high, low]


def right_list(value):
    high, middle, low = split(value)
    return [high, high, middle, middle, low, high]


def left_parts(value):
    return jnp.concatenate([part.astype(jnp.bfloat16) for part in left_list(value)], 1)


def right_parts(value):
    return jnp.concatenate([part.astype(jnp.bfloat16) for part in right_list(value)], 0)


def product(left, right):
    return jnp.dot(left, right, preferred_element_type=jnp.float32)


def inverse_kernel(
    core_ref, own_ref, other_ref, result_ref, out_ref, left_ref, right_ref, block_ref, done
):
    size = out_ref.shape[0]
    blocks = size // LANE
    tile = 256
    half = LANE // 2
    core = core_ref[0]
    row = lax.broadcasted_iota(jnp.int32, (LANE, LANE), 0)
    column = lax.broadcasted_iota(jnp.int32, (LANE, LANE), 1)
    diagonal = row == column
    for a in range(blocks):
        for d in range(STRIP):
            b = (a + d) % blocks
            place, source = slice(b * LANE, (b + 1) * LANE), slice(d * LANE, (d + 1) * LANE)
            for part_ref, index in ((own_ref, core), (other_ref, 1 - core)):
                rows = pl.ds(pl.multiple_of(a * LANE + index * half, half), half)
                out_ref[rows, place] = part_ref[a * half : (a + 1) * half, source]
    total = jnp.zeros((LANE, LANE), jnp.float32)
    for a in range(blocks):
        ours = slice(a * LANE, (a + 1) * LANE)
        total = total + jnp.where(diagonal, out_ref[ours, ours], 0.0)
        for d in range(1, blocks // 2):
            b = (a + d) % blocks
            theirs = slice(b * LANE, (b + 1) * LANE)
            out_ref[theirs, ours] = out_ref[ours, theirs].T
    ridge = damping * jnp.sum(total) / size
    for a in range(blocks):
        ours = slice(a * LANE, (a + 1) * LANE)
        out_ref[ours, ours] = out_ref[ours, ours] + jnp.where(diagonal, ridge, 0.0)

    def keep(rows):
        for r in range(LANE // SUB):
            block_ref[r * SUB : (r + 1) * SUB, :] = rows[r]

    keep(invert_block(out_ref[0:LANE, 0:LANE]))

    def pivot_rows(here, inverse):
        inverse_parts = left_parts(inverse)
        for m in range(size // tile):
            columns = slice(m * tile, (m + 1) * tile)
            scaled = product(inverse_parts, right_parts(out_ref[here, columns]))
            right_ref[:, columns] = right_parts(scaled)
            out_ref[here, columns] = scaled

    def step(k, carry):
        here = pl.ds(pl.multiple_of(k * LANE, LANE), LANE)
        after = pl.ds(pl.multiple_of((k + 1) * LANE, LANE), LANE)
        inverse = block_ref[...]
        ahead = product(left_parts(inverse), right_parts(out_ref[here, after]))
        following = out_ref[after, after] - product(
            left_parts(out_ref[after, here]), right_parts(ahead)
        )
        for m in range(blocks):
            rows = slice(m * LANE, (m + 1) * LANE)
            left_ref[rows, :] = left_parts(out_ref[rows, here])
        left_ref[here, :] = jnp.zeros((LANE, 6 * LANE), jnp.bfloat16)
        pivot_rows(here, inverse)
        out_ref[:, here] = jnp.zeros((size, LANE), jnp.float32)
        out_ref[here, here] = inverse
        right_ref[:, here] = right_parts(inverse)

        def update(p):
            m, n = divmod(p, size // tile)
            columns = slice(n * tile, (n + 1) * tile)
            rows = slice(m * tile, (m + 1) * tile)
            out_ref[rows, columns] = out_ref[rows, columns] - product(
                left_ref[rows, :], right_ref[:, columns]
            )

        keep(invert_block(following, update))
        return carry

    lax.fori_loop(0, blocks - 1, step, 0)
    end = size - LANE
    upper = pltpu.make_async_copy(out_ref.at[:end], result_ref.at[:end], done.at[0])
    upper.start()
    inverse = block_ref[...]
    pivot_rows(slice(end, size), inverse)
    out_ref[end:, end:] = inverse
    lower = pltpu.make_async_copy(out_ref.at[end:], result_ref.at[end:], done.at[1])
    lower.start()
    upper.wait()
    lower.wait()


WHOLE = pl.BlockSpec(memory_space=pltpu.VMEM)
OUTSIDE = pl.BlockSpec(memory_space=pltpu.HBM)
SCALARS = pl.BlockSpec(memory_space=pltpu.SMEM)
ROOM = pltpu.CompilerParams(vmem_limit_bytes=40 * 2**20)
MOST = pltpu.CompilerParams(vmem_limit_bytes=60 * 2**20)


def swept(core, own, other):
    size = 2 * own.shape[0]
    return pl.pallas_call(
        inverse_kernel,
        out_shape=jax.ShapeDtypeStruct((size, size), jnp.float32),
        in_specs=[SCALARS, WHOLE, WHOLE],
        out_specs=OUTSIDE,
        scratch_shapes=[
            pltpu.VMEM((size, size), jnp.float32),
            pltpu.VMEM((size, 6 * LANE), jnp.bfloat16),
            pltpu.VMEM((6 * LANE, size), jnp.bfloat16),
            pltpu.VMEM((LANE, LANE), jnp.float32),
            pltpu.SemaphoreType.DMA((2,)),
        ],
        compiler_params=MOST,
        cost_estimate=pl.CostEstimate(
            flops=12 * size**3, bytes_accessed=8 * size**2, transcendentals=0
        ),
    )(core, own, other)


def split_kernel(value_ref, high_ref, middle_ref, low_ref):
    for part_ref, part in zip((high_ref, middle_ref, low_ref), split(value_ref[...])):
        part_ref[...] = part.astype(jnp.bfloat16)


def split_rows(value):
    rows, width = value.shape
    tile = 128
    spec = pl.BlockSpec((tile, width), lambda n: (n, 0))
    part = jax.ShapeDtypeStruct(value.shape, jnp.bfloat16)
    return pl.pallas_call(
        split_kernel,
        grid=(rows // tile,),
        out_shape=(part,) * 3,
        in_specs=[spec],
        out_specs=(spec,) * 3,
        compiler_params=ROOM,
        cost_estimate=pl.CostEstimate(
            flops=8 * value.size, bytes_accessed=10 * value.size, transcendentals=0
        ),
    )(value)


def solve_kernel(own_ref, other_ref, high_ref, middle_ref, low_ref, out_ref):
    rows, width = out_ref.shape
    end = width - LANE

    def times(value, span, columns):
        left = [part.astype(jnp.bfloat16) for part in split(value)]
        by_high = product(jnp.concatenate(left, 0), high_ref[span, columns])
        by_middle = product(jnp.concatenate(left[:2], 0), middle_ref[span, columns])
        small = by_middle[rows:] + by_high[2 * rows :] + product(left[0], low_ref[span, columns])
        return by_high[:rows] + (by_high[rows : 2 * rows] + by_middle[:rows] + small)

    cross = own_ref[...] + other_ref[...]
    rest = cross[:, end:] - times(cross[:, :end], slice(0, end), slice(end, width))
    out_ref[:, end:] = times(rest, slice(end, width), slice(end, width))
    for start in range(0, end, LANE):
        columns = slice(start, start + LANE)
        out_ref[:, columns] = times(cross[:, :end], slice(0, end), columns) + times(
            rest, slice(end, width), columns
        )


def solve(own, other, parts):
    return pl.pallas_call(
        solve_kernel,
        out_shape=jax.ShapeDtypeStruct(own.shape, jnp.float32),
        in_specs=[WHOLE] * 5,
        out_specs=WHOLE,
        compiler_params=ROOM,
        cost_estimate=pl.CostEstimate(
            flops=12 * own.size * own.shape[1], bytes_accessed=7 * 2**20, transcendentals=0
        ),
    )(own, other, *parts)


def partial_kernel(place_ref, codes_ref, activations_ref, own_ref, other_ref, gram_ref, gram_other_ref, strip_ref):
    core, z = place_ref[0], place_ref[1]
    width = own_ref.shape[0]
    blocks = codes_ref.shape[1] // LANE
    half = LANE // 2
    low = codes_ref[...].astype(jnp.bfloat16)
    for part_ref, index in ((other_ref, 1 - core), (own_ref, core)):
        channels = activations_ref[:, pl.ds(pl.multiple_of(index * width, width), width)]
        part_ref[...] = contract(channels, low)

    def strip(d):
        start = pl.multiple_of(lax.rem(z + d, blocks) * LANE, LANE)
        return [part.astype(jnp.bfloat16) for part in split(codes_ref[:, pl.ds(start, LANE)])]

    ours = strip(0)
    for d in range(STRIP):
        theirs = ours if d == 0 else strip(d)
        terms = [contract(ours[i], theirs[j]) for i, j in ((2, 0), (0, 2), (1, 1), (1, 0), (0, 1), (0, 0))]
        strip_ref[:, d * LANE : (d + 1) * LANE] = functools.reduce(jnp.add, terms)
    gram_ref[...] = strip_ref[pl.ds(pl.multiple_of(core * half, half), half), :]
    gram_other_ref[...] = strip_ref[pl.ds(pl.multiple_of((1 - core) * half, half), half), :]


def contract(left, right):
    return lax.dot_general(left, right, (((0,), (0,)), ((), ())), preferred_element_type=jnp.float32)


def partial_terms(place, codes, activations):
    width = activations.shape[1] // 2
    moments = jax.ShapeDtypeStruct((width, codes.shape[1]), jnp.float32)
    gram = jax.ShapeDtypeStruct((LANE // 2, STRIP * LANE), jnp.float32)
    return pl.pallas_call(
        partial_kernel,
        out_shape=(moments, moments, gram, gram),
        in_specs=[SCALARS, WHOLE, WHOLE],
        out_specs=(WHOLE,) * 4,
        scratch_shapes=[pltpu.VMEM((LANE, STRIP * LANE), jnp.float32)],
        compiler_params=ROOM,
        cost_estimate=pl.CostEstimate(
            flops=5 * 10**8, bytes_accessed=4 * 2**20, transcendentals=0
        ),
    )(place, codes, activations)


def cross_kernel(core_ref, weight_ref, own_ref, other_ref, out_ref):
    width = own_ref.shape[0]
    rows = weight_ref.shape[0] // 16
    tile = 256
    core = core_ref[0]
    left = [
        weight_ref[:, pl.ds(pl.multiple_of(start * width, width), width)]
        for start in (core, 1 - core)
    ]
    left = jnp.concatenate(left, 1)
    for n in range(out_ref.shape[1] // tile):
        columns = slice(n * tile, (n + 1) * tile)
        parts = zip(split(own_ref[:, columns]), split(other_ref[:, columns]))
        result = tree_sum(
            [product(left, jnp.concatenate(pair, 0).astype(jnp.bfloat16)) for pair in parts]
        )
        for y in range(2):
            for z in range(8):
                source, target = (y * 8 + z) * rows, (z * 2 + y) * rows
                out_ref[target : target + rows, columns] = result[source : source + rows, :]


def cross_terms(core, weight, own, other):
    return pl.pallas_call(
        cross_kernel,
        out_shape=jax.ShapeDtypeStruct((weight.shape[0], own.shape[1]), jnp.float32),
        in_specs=[SCALARS, WHOLE, WHOLE, WHOLE],
        out_specs=WHOLE,
        compiler_params=ROOM,
        cost_estimate=pl.CostEstimate(
            flops=6 * weight.size * own.shape[1], bytes_accessed=8 * 2**20, transcendentals=0
        ),
    )(core, weight, own, other)


def exchange_sum(value, axes, count):
    received = lax.all_to_all(value, axes, 0, 0, tiled=True)
    return received.reshape(count, -1, value.shape[1]).sum(0)


def exchange_gather(value, axes, count):
    copies = jnp.broadcast_to(value[None], (count,) + value.shape)
    return lax.all_to_all(copies.reshape(-1, value.shape[1]), axes, 0, 0, tiled=True)


def swap(value, axis):
    return lax.ppermute(value, axis, [(0, 1), (1, 0)])


def halves(value, index):
    half = value.shape[0] // 2
    own = lax.dynamic_slice_in_dim(value, index * half, half, 0)
    return own, lax.dynamic_slice_in_dim(value, (1 - index) * half, half, 0)


def shards(activations, weight, basis):
    core, y_hi, z = (lax.axis_index(name) for name in ("core", "y_hi", "z"))
    partial_value = lax.dot_general(
        activations, basis, (((1,), (1,)), ((), ())), preferred_element_type=jnp.float32
    )
    codes = exchange_gather(exchange_sum(partial_value, CH, 16), CH, 16)

    here = core.astype(jnp.int32)[None]
    place = jnp.stack([core, z]).astype(jnp.int32)
    own, other, gram, gram_other = partial_terms(place, codes, activations)
    gram = gram + swap(gram_other, "core")
    own = own + swap(other, "core")
    gram = exchange_gather(exchange_sum(gram, PLANE, 8), PLANE, 8)
    own, gram = lax.optimization_barrier((own, gram))
    gram = lax.all_gather(gram, "z", axis=0, tiled=True)
    own = exchange_gather(exchange_sum(own, PLANE, 8), PLANE, 8)
    cross = cross_terms(here, weight, own, swap(own, "core"))
    cross, gram = lax.optimization_barrier((cross, gram))
    cross = lax.psum_scatter(cross, "z", scatter_dimension=0, tiled=True)
    inverse = swept(here, gram, swap(gram, "core"))
    cross, inverse = lax.optimization_barrier((cross, inverse))
    own, other = halves(cross, y_hi)
    return solve(own, swap(other, "y_hi"), split_rows(inverse))


def solution(mesh):
    names = tuple(name for name, _ in AXES)
    fine = Mesh(mesh.devices.reshape([size for _, size in AXES]), names)
    in_specs = (P(TOK, CH), P(TOK, CH), P(None, CH))
    out_specs = P(TOK + CH, None)
    return jax.shard_map(shards, mesh=fine, in_specs=in_specs, out_specs=out_specs, check_vma=False)
```

time: 240 us -> 224 us (0.933)
  blocking collectives: 85.4 us -> 65.9 us
  waiting for transfers between devices: 40.7 us -> 52 us
  matrix products: 8.07 us -> 1.41 us
  starting transfers between devices: 16.9 us -> 22.9 us
  local copies, waits for them, and re-layouts: 15.4 us -> 9.47 us
    all_to_all x3 -> x2, blocking collectives: 68.3 us -> 47.5 us  [exchange_sum(): received = lax.all_to_all(value, axes, 0, 0, tiled=True)]
    all_to_all x0 -> x1, waiting for transfers between devices: none -> 12.1 us  [exchange_sum(): received = lax.all_to_all(value, axes, 0, 0, tiled=True)]
    dot_general x3 -> x0, matrix products: 6.66 us -> none  [the longest x1 5.65 us: shards(): jnp.dot(cross, inverse, precision=lax.Precision.HIGHEST, preferred_elemen...]
    all_to_all x0 -> x1, starting transfers between devices: none -> 3.56 us  [exchange_sum(): received = lax.all_to_all(value, axes, 0, 0, tiled=True)]
    ppermute x3 -> x5, starting transfers between devices: 7 us -> 9.94 us  [swap(): return lax.ppermute(value, axis, [(0, 1), (1, 0)])]
    optimization_barrier x1 -> x0, local copies, waits for them, and re-layouts: 2.56 us -> none  [shards(): own, gram_rows = lax.optimization_barrier((own, gram_rows))]
    unnamed x18 -> x14, local copies, waits for them, and re-layouts: 8.79 us -> 6.5 us
    pallas_call x1 -> x4, Pallas kernels: 53.1 us -> 53.2 us  [the longest x1 46.8 us: swept(): pl.pallas_call(inverse_kernel, out_shape=jax.ShapeDtypeStruct((size, size...]
  transfers between devices with their start and end apart: 7 -> 10, of which waited for: 4 -> 7; matrix products, arithmetic and copies ran while one was open for 3% -> 1% of each run, Pallas kernels for 24% -> 23%
where the time goes in v3:
time: 224 us; the launch traced here: 223 us
  blocking collectives  65.9 us (29%)
  Pallas kernels  56.3 us (25%)
  waiting for transfers between devices  52 us (23%)
  starting transfers between devices  22.9 us (10%)
  between operations  13.5 us (6%)
  local copies, waits for them, and re-layouts  9.47 us (4%)
    all_to_all x2, blocking collectives, exchange_sum(): received = lax.all_to_all(value, axes, 0, 0, tiled=True)  47.5 us
    pallas_call x1, Pallas kernels, swept(): pl.pallas_call(inverse_kernel, out_shape=jax.ShapeDtypeStruct((size, size...  46.8 us
    all_to_all x2, waiting for transfers between devices, exchange_gather(): lax.all_to_all(copies.reshape(-1, value.shape[1]), axes, 0, 0, tiled=True)  29.9 us
    all_to_all x1, blocking collectives, exchange_gather(): lax.all_to_all(copies.reshape(-1, value.shape[1]), axes, 0, 0, tiled=True)  18.5 us
    all_to_all x1, waiting for transfers between devices, exchange_sum(): received = lax.all_to_all(value, axes, 0, 0, tiled=True)  12.1 us
    ppermute x5, starting transfers between devices, swap(): return lax.ppermute(value, axis, [(0, 1), (1, 0)])  9.94 us
    all_to_all x2, starting transfers between devices, exchange_gather(): lax.all_to_all(copies.reshape(-1, value.shape[1]), axes, 0, 0, tiled=True)  9.36 us
    ppermute x5, waiting for transfers between devices, swap(): return lax.ppermute(value, axis, [(0, 1), (1, 0)])  9.33 us
  transfers between devices with their start and end apart: 10, of which 7 were waited for; matrix products, arithmetic and copies ran while one was open for 1% of the time, Pallas kernels for 23%

profile of v3, /device:TPU:1, one launch (start us, length us, event | category | flops | bytes accessed | tf_op | source)
XLA Modules:
  0.0 223.0 jit_solution(8123973523509302223)
XLA Ops:
  6.5 1.2 copy-done
  7.8 1.4 fusion
  9.2 38.0 %all_to_all.52 = f32[16,16,1024]{2,1,0:T(8,128)S(1)} all-to-all(f32[16,16,1024]{2,1,0:T(8,128)S(1)} %bitcast.14), channel_id=1, replica_groups=mesh['x'=4,'y_lo'=2,'core'=2,'y_hi'=2,'z'=8] {'y_hi','z'}, dimensions={0} | all-to-all | bytes 2097152 | tf_op jit(solution)/shard_map/all_to_all | solution.py:378
  47.3 1.1 broadcast_in_dim.9
  48.4 6.0 %all-to-all-start.1 = ((f32[16,16,1024]{2,1,0:T(8,128)}), f32[16,16,1024]{2,1,0:T(8,128)S(1)}, u32[]{:S(2)}, u32[]{:S(2)}) async-start(f32[16,16,1024]{2,1,0:T(8,128)} %broadcast_in_dim.9), calls=%async_computation.1 | async-start | bytes 2097152 | tf_op jit(solution)/shard_map/all_to_all | solution.py:384
  54.4 25.7 %all-to-all-done.1 = f32[16,16,1024]{2,1,0:T(8,128)S(1)} async-done(((f32[16,16,1024]{2,1,0:T(8,128)}), f32[16,16,1024]{2,1,0:T(8,128)S(1)}, u32[]{:S(2)}, u32[]{:S(2)}) %all-to-all-start.1) | async-done | bytes 1048608 | tf_op jit(solution)/shard_map/all_to_all | solution.py:384
  80.1 2.1 shard_map.37
  82.2 2.9 %collective-permute-start = (f32[256,1024]{1,0:T(8,128)}, f32[256,1024]{1,0:T(8,128)S(1)}, u32[]{:S(2)}, u32[]{:S(2)}) collective-permute-start(f32[256,1024]{1,0:T(8,128)} %get-tuple-element.19), channel_id=1, source_target_pairs={{0,16},{16,0},{1,17},{17,1},{2,18},{18,2},{3,19},{19,3},{4,20},{20... | collective-permute-start | bytes 3145736 | tf_op jit(solution)/shard_map/ppermute | solution.py:388
  85.1 2.4 %collective-permute-done.1 = f32[64,640]{1,0:T(8,128)S(1)} collective-permute-done((f32[64,640]{1,0:T(8,128)S(1)}, f32[64,640]{1,0:T(8,128)S(1)}, u32[]{:S(2)}, u32[]{:S(2)}) %collective-permute-start.1) | collective-permute-done | bytes 163872 | tf_op jit(solution)/shard_map/ppermute | solution.py:388
  87.5 9.4 %all_to_all.53 = f32[8,8,640]{2,1,0:T(8,128)S(1)} all-to-all(f32[8,8,640]{2,1,0:T(8,128)S(1)} %add_bitcast_fusion), channel_id=1, replica_groups=mesh['x'=4,'y_lo'=2,'core'=2,'y_hi'=2,'z'=8] {'x','y_lo'}, dimensions={0} | all-to-all | bytes 327680 | tf_op jit(solution)/shard_map/all_to_all | solution.py:378
  97.0 0.7 broadcast_in_dim.10
  97.7 3.4 %all-to-all-start.3 = ((f32[8,8,640]{2,1,0:T(8,128)}), f32[8,8,640]{2,1,0:T(8,128)S(1)}, u32[]{:S(2)}, u32[]{:S(2)}) async-start(f32[8,8,640]{2,1,0:T(8,128)} %broadcast_in_dim.10), calls=%async_computation.3 | async-start | bytes 327680 | tf_op jit(solution)/shard_map/all_to_all | solution.py:384
  101.1 1.1 add.14
  102.2 4.2 %all-to-all-done.3 = f32[8,8,640]{2,1,0:T(8,128)S(1)} async-done(((f32[8,8,640]{2,1,0:T(8,128)}), f32[8,8,640]{2,1,0:T(8,128)S(1)}, u32[]{:S(2)}, u32[]{:S(2)}) %all-to-all-start.3) | async-done | bytes 163872 | tf_op jit(solution)/shard_map/all_to_all | solution.py:384
  106.4 3.6 %all-to-all-start.4 = ((f32[8,32,1024]{2,1,0:T(8,128)}), f32[8,32,1024]{2,1,0:T(8,128)S(1)}, u32[]{:S(2)}, u32[]{:S(2)}) async-start(f32[8,32,1024]{2,1,0:T(8,128)} %bitcast.6), calls=%async_computation.4 | async-start | bytes 2097152 | tf_op jit(solution)/shard_map/all_to_all | solution.py:378
  110.0 0.7 all-gather.2.cloned.1.call-update
  110.7 12.1 %all-to-all-done.4 = f32[8,32,1024]{2,1,0:T(8,128)S(1)} async-done(((f32[8,32,1024]{2,1,0:T(8,128)}), f32[8,32,1024]{2,1,0:T(8,128)S(1)}, u32[]{:S(2)}, u32[]{:S(2)}) %all-to-all-start.4) | async-done | bytes 1048608 | tf_op jit(solution)/shard_map/all_to_all | solution.py:378
  123.0 18.5 %all_to_all.54 = f32[8,32,1024]{2,1,0:T(8,128)S(1)} all-to-all(f32[8,32,1024]{2,1,0:T(8,128)S(1)} %broadcast_in_dim.11), channel_id=1, replica_groups=mesh['x'=4,'y_lo'=2,'core'=2,'y_hi'=2,'z'=8] {'x','y_lo'}, dimensions={0} | all-to-all | bytes 2097152 | tf_op jit(solution)/shard_map/all_to_all | solution.py:384
  141.5 2.7 %collective-permute-start.2 = (f32[256,1024]{1,0:T(8,128)S(1)}, f32[256,1024]{1,0:T(8,128)S(1)}, u32[]{:S(2)}, u32[]{:S(2)}) collective-permute-start(f32[256,1024]{1,0:T(8,128)S(1)} %bitcast.12), channel_id=1, source_target_pairs={{0,16},{16,0},{1,17},{17,1},{2,18},{18,2},{3,19},{19,3},{4,20},{20... | collective-permute-start | bytes 3145736 | tf_op jit(solution)/shard_map/ppermute | solution.py:388
  144.1 2.3 %collective-permute-done.2.other_ref = f32[256,1024]{1,0:T(8,128)S(1)} collective-permute-done((f32[256,1024]{1,0:T(8,128)S(1)}, f32[256,1024]{1,0:T(8,128)S(1)}, u32[]{:S(2)}, u32[]{:S(2)}) %collective-permute-start.2) | collective-permute-done | bytes 1048608 | tf_op jit(solution)/shard_map/ppermute | solution.py:388
  146.4 3.1 %shard_map.38 = f32[896,1024]{1,0:T(8,128)S(1)} custom-call(s32[1]{0:T(128)} %bitcast.core_ref, bf16[896,512]{1,0:T(8,128)(2,1)S(1)} %copy-done.4, f32[256,1024]{1,0:T(8,128)S(1)} %bitcast.13, f32[256,1024]{1,0:T(8,128)S(1)} %collective-permute-done.2.other_ref), custom_call_target="tpu_custom_call" | custom-call | flops 2818572288 | bytes 8388608 | tf_op jit(solution)/shard_map/pallas_call | solution.py:365
  149.5 1.8 copy-done.2
  151.3 1.3 copy-done.6
  152.6 1.6 collective-permute-start.3
  154.2 2.8 %collective-permute-done.3.other_ref = f32[512,640]{1,0:T(8,128)} collective-permute-done((f32[512,640]{1,0:T(8,128)S(1)}, f32[512,640]{1,0:T(8,128)}, u32[]{:S(2)}, u32[]{:S(2)}) %collective-permute-start.3) | collective-permute-done | bytes 1310752 | tf_op jit(solution)/shard_map/ppermute | solution.py:388
  157.0 46.8 %shard_map.39.value_ref = f32[1024,1024]{1,0:T(8,128)} custom-call(s32[1]{0:T(128)} %bitcast.core_ref, f32[512,640]{1,0:T(8,128)} %all-gather.2.cloned.1.call-done.own_ref, f32[512,640]{1,0:T(8,128)} %collective-permute-done.3.other_ref), custom_call_target="tpu_custom_call" | custom-call | flops 12884901888 | bytes 8388608 | tf_op jit(solution)/shard_map/pallas_call | solution.py:222
  203.8 1.1 constant_dynamic-slice_fusion
  204.9 2.8 %collective-permute-start.4 = (f32[56,1024]{1,0:T(8,128)S(1)}, f32[56,1024]{1,0:T(8,128)S(1)}, u32[]{:S(2)}, u32[]{:S(2)}) collective-permute-start(f32[56,1024]{1,0:T(8,128)S(1)} %get-tuple-element.31), channel_id=1, source_target_pairs={{0,8},{8,0},{1,9},{9,1},{2,10},{10,2},{3,11},{11,3},{4,12},{12,4},... | collective-permute-start | bytes 688136 | tf_op jit(solution)/shard_map/ppermute | solution.py:388
  207.7 2.2 copy-done.1
  209.9 1.3 shard_map.40
  211.2 1.9 collective-permute-done.4.other_ref
  213.1 3.1 %shard_map.41 = f32[56,1024]{1,0:T(8,128)} custom-call(f32[56,1024]{1,0:T(8,128)S(1)} %get-tuple-element.32.own_ref, f32[56,1024]{1,0:T(8,128)S(1)} %collective-permute-done.4.other_ref, bf16[1024,1024]{1,0:T(8,128)(2,1)S(1)} %get-tuple-element.28.high_ref, bf16[1024,1024]{1,0:T(8,128)(2,1)S(1)} %get-tuple-element.29.middle_ref, ...), custom_call_target="tpu_custom_call" | custom-call | flops 704643072 | bytes 7340032 | tf_op jit(solution)/shard_map/pallas_call | solution.py:286
  (23 shorter events, 0.5 us)
Async XLA Ops:
  6.5 1.2 copy-start
  47.2 32.9 %copy-start.3 = (bf16[256,512]{1,0:T(8,128)(2,1)S(1)}, bf16[256,512]{1,0:T(8,128)(2,1)}, u32[]{:S(2)}) copy-start(bf16[256,512]{1,0:T(8,128)(2,1)} %activations_ref.1) | copy-start | bytes 786436
  48.4 31.8 %all-to-all-start.1 = ((f32[16,16,1024]{2,1,0:T(8,128)}), f32[16,16,1024]{2,1,0:T(8,128)S(1)}, u32[]{:S(2)}, u32[]{:S(2)}) async-start(f32[16,16,1024]{2,1,0:T(8,128)} %broadcast_in_dim.9), calls=%async_computation.1 | async-start | bytes 2097152 | tf_op jit(solution)/shard_map/all_to_all | solution.py:384
  82.2 18.8 %collective-permute-start = (f32[256,1024]{1,0:T(8,128)}, f32[256,1024]{1,0:T(8,128)S(1)}, u32[]{:S(2)}, u32[]{:S(2)}) collective-permute-start(f32[256,1024]{1,0:T(8,128)} %get-tuple-element.19), channel_id=1, source_target_pairs={{0,16},{16,0},{1,17},{17,1},{2,18},{18,2},{3,19},{19,3},{4,20},{20... | collective-permute-start | bytes 3145736 | tf_op jit(solution)/shard_map/ppermute | solution.py:388
  85.1 2.4 %collective-permute-start.1 = (f32[64,640]{1,0:T(8,128)S(1)}, f32[64,640]{1,0:T(8,128)S(1)}, u32[]{:S(2)}, u32[]{:S(2)}) collective-permute-start(f32[64,640]{1,0:T(8,128)S(1)} %get-tuple-element.21), channel_id=1, source_target_pairs={{0,16},{16,0},{1,17},{17,1},{2,18},{18,2},{3,19},{19,3},{4,20},{20... | collective-permute-start | bytes 491528 | tf_op jit(solution)/shard_map/ppermute | solution.py:388
  97.7 8.7 %all-to-all-start.3 = ((f32[8,8,640]{2,1,0:T(8,128)}), f32[8,8,640]{2,1,0:T(8,128)S(1)}, u32[]{:S(2)}, u32[]{:S(2)}) async-start(f32[8,8,640]{2,1,0:T(8,128)} %broadcast_in_dim.10), calls=%async_computation.3 | async-start | bytes 327680 | tf_op jit(solution)/shard_map/all_to_all | solution.py:384
  106.4 3.6 %copy-start.5 = (f32[8,8,640]{2,1,0:T(8,128)}, f32[8,8,640]{2,1,0:T(8,128)S(1)}, u32[]{:S(2)}) copy-start(f32[8,8,640]{2,1,0:T(8,128)S(1)} %all-to-all-done.3) | copy-start | bytes 491524
  106.4 16.5 %all-to-all-start.4 = ((f32[8,32,1024]{2,1,0:T(8,128)}), f32[8,32,1024]{2,1,0:T(8,128)S(1)}, u32[]{:S(2)}, u32[]{:S(2)}) async-start(f32[8,32,1024]{2,1,0:T(8,128)} %bitcast.6), calls=%async_computation.4 | async-start | bytes 2097152 | tf_op jit(solution)/shard_map/all_to_all | solution.py:378
  109.9 41.4 %all-gather.2.cloned.1.call-start = ((), (), s32[]{:S(2)}) async-start(), calls=%async_computation.7 | async-start | bytes 1474560 | tf_op jit(solution)/shard_map/all_gather | solution.py:411
  110.7 35.8 %copy-start.4 = (bf16[896,512]{1,0:T(8,128)(2,1)S(1)}, bf16[896,512]{1,0:T(8,128)(2,1)}, u32[]{:S(2)}) copy-start(bf16[896,512]{1,0:T(8,128)(2,1)} %weight_ref.1) | copy-start | bytes 2752516
  110.7 93.1 %reduce-scatter.2.cloned.1.call-start = ((), (), s32[]{:S(2)}) async-start(), calls=%async_computation.8 | async-start | bytes 4128768 | tf_op jit(solution)/shard_map/reduce_scatter | solution.py:415
  141.5 5.0 %collective-permute-start.2 = (f32[256,1024]{1,0:T(8,128)S(1)}, f32[256,1024]{1,0:T(8,128)S(1)}, u32[]{:S(2)}, u32[]{:S(2)}) collective-permute-start(f32[256,1024]{1,0:T(8,128)S(1)} %bitcast.12), channel_id=1, source_target_pairs={{0,16},{16,0},{1,17},{17,1},{2,18},{18,2},{3,19},{19,3},{4,20},{20... | collective-permute-start | bytes 3145736 | tf_op jit(solution)/shard_map/ppermute | solution.py:388
  149.5 1.8 copy-start.2
  151.3 1.3 copy-start.6
  152.6 4.3 %collective-permute-start.3 = (f32[512,640]{1,0:T(8,128)S(1)}, f32[512,640]{1,0:T(8,128)}, u32[]{:S(2)}, u32[]{:S(2)}) collective-permute-start(f32[512,640]{1,0:T(8,128)S(1)} %copy-done.6), channel_id=1, source_target_pairs={{0,16},{16,0},{1,17},{17,1},{2,18},{18,2},{3,19},{19,3},{4,20},{20... | collective-permute-start | bytes 3932168 | tf_op jit(solution)/shard_map/ppermute | solution.py:388
  204.9 8.2 %collective-permute-start.4 = (f32[56,1024]{1,0:T(8,128)S(1)}, f32[56,1024]{1,0:T(8,128)S(1)}, u32[]{:S(2)}, u32[]{:S(2)}) collective-permute-start(f32[56,1024]{1,0:T(8,128)S(1)} %get-tuple-element.31), channel_id=1, source_target_pairs={{0,8},{8,0},{1,9},{9,1},{2,10},{10,2},{3,11},{11,3},{4,12},{12,4},... | collective-permute-start | bytes 688136 | tf_op jit(solution)/shard_map/ppermute | solution.py:388
  207.7 2.2 copy-start.1
Sparse Core Ops, SparseCore 0:
  112.6 35.3 all-gather.1
  151.5 52.2 reduce-scatter.1

commit v4 on v3

--- a/solution.py
+++ b/solution.py
@@ -11,7 +11,6 @@
 damping = 0.1
 
 SUB, LANE = 8, 128
-NEAR = 1
 STRIP = 5
 AXES = (("x", 4), ("y_lo", 2), ("core", 2), ("y_hi", 2), ("z", 8))
 TOK = ("x", "y_lo", "core")
@@ -46,11 +45,17 @@
     return {place: -value for place, value in entry.items()}
 
 
-def eliminate(near, pivot):
-    return tree_sum([near[j] * spread(pivot[j : j + 1, :]) for j in range(SUB)])
-
-
-def invert_block(block, between=None):
+def combine(columns, rows):
+    return tree_sum([column * row for column, row in zip(columns, rows)])
+
+
+def pick(sub, values):
+    pairs = [jnp.where(sub == i, values[i], values[i + 1]) for i in range(0, SUB, 2)]
+    low, high = jnp.where(sub < 2, *pairs[:2]), jnp.where(sub < 6, *pairs[2:])
+    return jnp.where(sub < 4, low, high)
+
+
+def invert_block(block, buffer, between=None):
     sub = lax.broadcasted_iota(jnp.int32, (SUB, LANE), 0)
     lane = lax.broadcasted_iota(jnp.int32, (SUB, LANE), 1)
     panels = LANE // SUB
@@ -59,23 +64,23 @@
         base = p * SUB
         panel = rows[p]
         inside = (lane >= base) & (lane < base + SUB)
-
-        def columns_of(r):
-            return [spread(rows[r][:, base + j : base + j + 1]) for j in range(SUB)]
-
-        columns = columns_of(p)
-        near = {r: columns_of(r) for r in range(p + 1, min(p + 1 + NEAR, panels))}
-        small = invert_small(
-            {(i, j): spread(columns[j][i : i + 1, :]) for j in range(SUB) for i in range(j + 1)}
-        )
-        small_columns = []
-        for j in range(SUB):
-            column = small[0, j]
-            for i in range(1, SUB):
-                column = jnp.where(sub == i, small[min(i, j), max(i, j)], column)
-            small_columns.append(column)
+        offset = (p % 2) * (SUB + 2) * SUB
+
+        def rows_of(slot, value):
+            start = offset + slot * SUB
+            buffer[start : start + SUB, :] = value
+            return [spread(buffer[start + i : start + i + 1, :]) for i in range(SUB)]
+
+        def columns_of(value):
+            return [spread(value[:, base + j : base + j + 1]) for j in range(SUB)]
+
+        entries = [rows_of(j, column) for j, column in enumerate(columns_of(panel))]
+        small = invert_small({(i, j): entries[j][i] for j in range(SUB) for i in range(j + 1)})
+        small_columns = [
+            pick(sub, [small[min(i, j), max(i, j)] for i in range(SUB)]) for j in range(SUB)
+        ]
         wide = jnp.where(inside, jnp.where(lane - base == sub, 1.0, 0.0), panel)
-        pivot = eliminate(small_columns, wide)
+        pivot = combine(small_columns, rows_of(SUB, wide))
         left = jnp.concatenate(left_list(jnp.where(lane < base, -panel, panel)), 0)
         right = jnp.concatenate(right_list(pivot), 0)
         change = lax.dot_general(
@@ -85,10 +90,12 @@
             preferred_element_type=jnp.float32,
         )
         for r in range(panels):
-            if r in near:
-                rows[r] = jnp.where(inside, 0.0, rows[r]) - eliminate(near[r], pivot)
-            elif r != p:
-                rows[r] = jnp.where(inside, 0.0, rows[r]) - change[r * SUB : (r + 1) * SUB, :]
+            if r == p + 1:
+                amount = combine(columns_of(rows[r]), rows_of(SUB + 1, pivot))
+            else:
+                amount = change[r * SUB : (r + 1) * SUB, :]
+            if r != p:
+                rows[r] = jnp.where(inside, 0.0, rows[r]) - amount
         rows[p] = pivot
         if between is not None:
             between(p)
@@ -125,7 +132,7 @@
 
 
 def inverse_kernel(
-    core_ref, own_ref, other_ref, result_ref, out_ref, left_ref, right_ref, block_ref, done
+    core_ref, own_ref, other_ref, result_ref, out_ref, left_ref, right_ref, block_ref, buffer, done
 ):
     size = out_ref.shape[0]
     blocks = size // LANE
@@ -159,7 +166,7 @@
         for r in range(LANE // SUB):
             block_ref[r * SUB : (r + 1) * SUB, :] = rows[r]
 
-    keep(invert_block(out_ref[0:LANE, 0:LANE]))
+    keep(invert_block(out_ref[0:LANE, 0:LANE], buffer))
 
     def pivot_rows(here, inverse):
         inverse_parts = left_parts(inverse)
@@ -194,7 +201,7 @@
                 left_ref[rows, :], right_ref[:, columns]
             )
 
-        keep(invert_block(following, update))
+        keep(invert_block(following, buffer, update))
         return carry
 
     lax.fori_loop(0, blocks - 1, step, 0)
@@ -229,6 +236,7 @@
             pltpu.VMEM((size, 6 * LANE), jnp.bfloat16),
             pltpu.VMEM((6 * LANE, size), jnp.bfloat16),
             pltpu.VMEM((LANE, LANE), jnp.float32),
+            pltpu.VMEM((2 * (SUB + 2) * SUB, LANE), jnp.float32),
             pltpu.SemaphoreType.DMA((2,)),
         ],
         compiler_params=MOST,
@@ -273,13 +281,17 @@
         return by_high[:rows] + (by_high[rows : 2 * rows] + by_middle[:rows] + small)
 
     cross = own_ref[...] + other_ref[...]
-    rest = cross[:, end:] - times(cross[:, :end], slice(0, end), slice(end, width))
-    out_ref[:, end:] = times(rest, slice(end, width), slice(end, width))
-    for start in range(0, end, LANE):
-        columns = slice(start, start + LANE)
-        out_ref[:, columns] = times(cross[:, :end], slice(0, end), columns) + times(
-            rest, slice(end, width), columns
-        )
+    tile = 2 * LANE
+    upper, lower = slice(0, end), slice(end, width)
+    final = slice(width - tile, width)
+    early = times(cross[:, :end], upper, final)
+    rest = cross[:, end:] - early[:, LANE:]
+    late = times(rest, lower, final)
+    out_ref[:, width - tile : end] = early[:, :LANE] + late[:, :LANE]
+    out_ref[:, end:] = late[:, LANE:]
+    for start in range(0, width - tile, tile):
+        columns = slice(start, start + tile)
+        out_ref[:, columns] = times(cross[:, :end], upper, columns) + times(rest, lower, columns)
 
 
 def solve(own, other, parts):
@@ -339,39 +351,41 @@
     )(place, codes, activations)
 
 
-def cross_kernel(core_ref, weight_ref, own_ref, other_ref, out_ref):
-    width = own_ref.shape[0]
+def cross_kernel(place_ref, weight_ref, part_ref, *refs):
+    out_ref = refs[-1]
+    width = part_ref.shape[0]
     rows = weight_ref.shape[0] // 16
     tile = 256
-    core = core_ref[0]
-    left = [
-        weight_ref[:, pl.ds(pl.multiple_of(start * width, width), width)]
-        for start in (core, 1 - core)
-    ]
-    left = jnp.concatenate(left, 1)
+    core, y_hi = place_ref[0], place_ref[1]
+    left = weight_ref[:, pl.ds(pl.multiple_of(core * width, width), width)]
     for n in range(out_ref.shape[1] // tile):
         columns = slice(n * tile, (n + 1) * tile)
-        parts = zip(split(own_ref[:, columns]), split(other_ref[:, columns]))
         result = tree_sum(
-            [product(left, jnp.concatenate(pair, 0).astype(jnp.bfloat16)) for pair in parts]
+            [product(left, part.astype(jnp.bfloat16)) for part in split(part_ref[:, columns])]
         )
         for y in range(2):
+            offset = lax.rem(y + y_hi, 2) * rows
             for z in range(8):
-                source, target = (y * 8 + z) * rows, (z * 2 + y) * rows
-                out_ref[target : target + rows, columns] = result[source : source + rows, :]
-
-
-def cross_terms(core, weight, own, other):
+                source = (y * 8 + z) * rows
+                value = result[source : source + rows, :]
+                target = pl.ds(pl.multiple_of(z * 2 * rows + offset, SUB), rows)
+                for earlier in refs[:-1]:
+                    value = value + earlier[target, columns]
+                out_ref[target, columns] = value
+
+
+def cross_terms(core, y_hi, weight, part, *earlier):
+    place = jnp.stack([core, y_hi]).astype(jnp.int32)
     return pl.pallas_call(
         cross_kernel,
-        out_shape=jax.ShapeDtypeStruct((weight.shape[0], own.shape[1]), jnp.float32),
-        in_specs=[SCALARS, WHOLE, WHOLE, WHOLE],
+        out_shape=jax.ShapeDtypeStruct((weight.shape[0], part.shape[1]), jnp.float32),
+        in_specs=[SCALARS] + [WHOLE] * (2 + len(earlier)),
         out_specs=WHOLE,
         compiler_params=ROOM,
         cost_estimate=pl.CostEstimate(
-            flops=6 * weight.size * own.shape[1], bytes_accessed=8 * 2**20, transcendentals=0
+            flops=3 * weight.size * part.shape[1], bytes_accessed=8 * 2**20, transcendentals=0
         ),
-    )(core, weight, own, other)
+    )(place, weight, part, *earlier)
 
 
 def exchange_sum(value, axes, count):
@@ -386,12 +400,6 @@
 
 def swap(value, axis):
     return lax.ppermute(value, axis, [(0, 1), (1, 0)])
-
-
-def halves(value, index):
-    half = value.shape[0] // 2
-    own = lax.dynamic_slice_in_dim(value, index * half, half, 0)
-    return own, lax.dynamic_slice_in_dim(value, (1 - index) * half, half, 0)
 
 
 def shards(activations, weight, basis):
@@ -407,16 +415,19 @@
     gram = gram + swap(gram_other, "core")
     own = own + swap(other, "core")
     gram = exchange_gather(exchange_sum(gram, PLANE, 8), PLANE, 8)
+    gram = jnp.concatenate([gram, gram], 1)
     own, gram = lax.optimization_barrier((own, gram))
     gram = lax.all_gather(gram, "z", axis=0, tiled=True)
     own = exchange_gather(exchange_sum(own, PLANE, 8), PLANE, 8)
-    cross = cross_terms(here, weight, own, swap(own, "core"))
+    cross = cross_terms(core, y_hi, weight, own)
+    cross = cross_terms(1 - core, y_hi, weight, swap(own, "core"), cross)
     cross, gram = lax.optimization_barrier((cross, gram))
     cross = lax.psum_scatter(cross, "z", scatter_dimension=0, tiled=True)
+    gram = gram[:, : STRIP * LANE]
     inverse = swept(here, gram, swap(gram, "core"))
     cross, inverse = lax.optimization_barrier((cross, inverse))
-    own, other = halves(cross, y_hi)
-    return solve(own, swap(other, "y_hi"), split_rows(inverse))
+    half = cross.shape[0] // 2
+    return solve(cross[:half], swap(cross[half:], "y_hi"), split_rows(inverse))
 
 
 def solution(mesh):

time: 224 us -> 218 us (0.973)
  waiting for transfers between devices: 52 us -> 32.8 us
  blocking collectives: 65.9 us -> 83.9 us
  starting transfers between devices: 22.9 us -> 18.1 us
    all_to_all x2 -> x3, blocking collectives: 47.5 us -> 62.4 us  [exchange_sum(): received = lax.all_to_all(value, axes, 0, 0, tiled=True)]
    all_to_all x1 -> x0, waiting for transfers between devices: 12.1 us -> none  [exchange_sum(): received = lax.all_to_all(value, axes, 0, 0, tiled=True)]
    all_to_all x2 -> x1, waiting for transfers between devices: 29.9 us -> 25.6 us  [exchange_gather(): lax.all_to_all(copies.reshape(-1, value.shape[1]), axes, 0, 0, tiled=True)]
    all_to_all x1 -> x0, starting transfers between devices: 3.56 us -> none  [exchange_sum(): received = lax.all_to_all(value, axes, 0, 0, tiled=True)]
    all_to_all x2 -> x1, starting transfers between devices: 9.36 us -> 5.98 us  [exchange_gather(): lax.all_to_all(copies.reshape(-1, value.shape[1]), axes, 0, 0, tiled=True)]
    all_to_all x1 -> x2, blocking collectives: 18.5 us -> 21.5 us  [exchange_gather(): lax.all_to_all(copies.reshape(-1, value.shape[1]), axes, 0, 0, tiled=True)]
    slice x0 -> x2, local copies, waits for them, and re-layouts: none -> 2.48 us  [the longest x1 1.4 us: shards(): gram = gram[:, :STRIP * LANE]]
    ppermute x5, waiting for transfers between devices: 9.33 us -> 6.92 us  [swap(): return lax.ppermute(value, axis, [(0, 1), (1, 0)])]
  transfers between devices with their start and end apart: 10 -> 8, of which waited for: 7 -> 6; matrix products, arithmetic and copies ran while one was open for 1% -> 1% of each run, Pallas kernels for 23% -> 23%
where the time goes in v4:
time: 218 us
  blocking collectives  83.9 us (38%)
  Pallas kernels  55.4 us (25%)
  waiting for transfers between devices  32.8 us (15%)
  starting transfers between devices  18.1 us (8%)
  between operations  13.5 us (6%)
  local copies, waits for them, and re-layouts  9.96 us (5%)
  other arithmetic  2.51 us (1%)
    all_to_all x3, blocking collectives, exchange_sum(): received = lax.all_to_all(value, axes, 0, 0, tiled=True)  62.4 us
    pallas_call x1, Pallas kernels, swept(): pl.pallas_call(inverse_kernel, out_shape=jax.ShapeDtypeStruct((size, size...  44.8 us
    all_to_all x1, waiting for transfers between devices, exchange_gather(): lax.all_to_all(copies.reshape(-1, value.shape[1]), axes, 0, 0, tiled=True)  25.6 us
    all_to_all x2, blocking collectives, exchange_gather(): lax.all_to_all(copies.reshape(-1, value.shape[1]), axes, 0, 0, tiled=True)  21.5 us
    ppermute x5, starting transfers between devices, swap(): return lax.ppermute(value, axis, [(0, 1), (1, 0)])  12 us
    ppermute x5, waiting for transfers between devices, swap(): return lax.ppermute(value, axis, [(0, 1), (1, 0)])  6.92 us
    unnamed x14, local copies, waits for them, and re-layouts  6.26 us
    all_to_all x1, starting transfers between devices, exchange_gather(): lax.all_to_all(copies.reshape(-1, value.shape[1]), axes, 0, 0, tiled=True)  5.98 us
  transfers between devices with their start and end apart: 8, of which 6 were waited for; matrix products, arithmetic and copies ran while one was open for 1% of the time, Pallas kernels for 23%

profile of v4, /device:TPU:1, one launch (start us, length us, event | category | flops | bytes accessed | tf_op | source)
XLA Modules:
  0.0 217.6 jit_solution(10687674051017757888)
XLA Ops:
  6.5 1.2 copy-done
  7.8 1.4 fusion.1
  9.2 38.0 %all_to_all.52 = f32[16,16,1024]{2,1,0:T(8,128)S(1)} all-to-all(f32[16,16,1024]{2,1,0:T(8,128)S(1)} %bitcast.17), channel_id=1, replica_groups=mesh['x'=4,'y_lo'=2,'core'=2,'y_hi'=2,'z'=8] {'y_hi','z'}, dimensions={0} | all-to-all | bytes 2097152 | tf_op jit(solution)/shard_map/all_to_all | solution.py:392
  47.3 1.1 broadcast_in_dim.6
  48.4 6.0 %all-to-all-start.1 = ((f32[16,16,1024]{2,1,0:T(8,128)}), f32[16,16,1024]{2,1,0:T(8,128)S(1)}, u32[]{:S(2)}, u32[]{:S(2)}) async-start(f32[16,16,1024]{2,1,0:T(8,128)} %broadcast_in_dim.6), calls=%async_computation.1 | async-start | bytes 2097152 | tf_op jit(solution)/shard_map/all_to_all | solution.py:398
  54.5 25.6 %all-to-all-done.1 = f32[16,16,1024]{2,1,0:T(8,128)S(1)} async-done(((f32[16,16,1024]{2,1,0:T(8,128)}), f32[16,16,1024]{2,1,0:T(8,128)S(1)}, u32[]{:S(2)}, u32[]{:S(2)}) %all-to-all-start.1) | async-done | bytes 1048608 | tf_op jit(solution)/shard_map/all_to_all | solution.py:398
  80.1 2.1 shard_map.37
  82.2 2.9 %collective-permute-start = (f32[256,1024]{1,0:T(8,128)}, f32[256,1024]{1,0:T(8,128)}, u32[]{:S(2)}, u32[]{:S(2)}) collective-permute-start(f32[256,1024]{1,0:T(8,128)} %get-tuple-element.19), channel_id=1, source_target_pairs={{0,16},{16,0},{1,17},{17,1},{2,18},{18,2},{3,19},{19,3},{4,20},{20... | collective-permute-start | bytes 3145736 | tf_op jit(solution)/shard_map/ppermute | solution.py:402
  85.1 2.4 %collective-permute-done.1 = f32[64,640]{1,0:T(8,128)S(1)} collective-permute-done((f32[64,640]{1,0:T(8,128)S(1)}, f32[64,640]{1,0:T(8,128)S(1)}, u32[]{:S(2)}, u32[]{:S(2)}) %collective-permute-start.1) | collective-permute-done | bytes 163872 | tf_op jit(solution)/shard_map/ppermute | solution.py:402
  87.5 9.4 %all_to_all.53 = f32[8,8,640]{2,1,0:T(8,128)S(1)} all-to-all(f32[8,8,640]{2,1,0:T(8,128)S(1)} %add_bitcast_fusion), channel_id=1, replica_groups=mesh['x'=4,'y_lo'=2,'core'=2,'y_hi'=2,'z'=8] {'x','y_lo'}, dimensions={0} | all-to-all | bytes 327680 | tf_op jit(solution)/shard_map/all_to_all | solution.py:392
  97.0 7.9 %all_to_all.54 = f32[8,8,640]{2,1,0:T(8,128)S(1)} all-to-all(f32[8,8,640]{2,1,0:T(8,128)S(1)} %broadcast_in_dim.7), channel_id=1, replica_groups=mesh['x'=4,'y_lo'=2,'core'=2,'y_hi'=2,'z'=8] {'x','y_lo'}, dimensions={0} | all-to-all | bytes 327680 | tf_op jit(solution)/shard_map/all_to_all | solution.py:398
  104.9 0.8 pad_maximum_fusion
  105.6 1.4 add.8
  107.1 15.0 %all_to_all.55 = f32[8,32,1024]{2,1,0:T(8,128)S(1)} all-to-all(f32[8,32,1024]{2,1,0:T(8,128)S(1)} %bitcast.16), channel_id=1, replica_groups=mesh['x'=4,'y_lo'=2,'core'=2,'y_hi'=2,'z'=8] {'x','y_lo'}, dimensions={0} | all-to-all | bytes 2097152 | tf_op jit(solution)/shard_map/all_to_all | solution.py:392
  122.1 0.1 broadcast_in_dim.8
  122.2 13.6 %all_to_all.56 = f32[8,32,1024]{2,1,0:T(8,128)S(1)} all-to-all(f32[8,32,1024]{2,1,0:T(8,128)S(1)} %broadcast_in_dim.8), channel_id=1, replica_groups=mesh['x'=4,'y_lo'=2,'core'=2,'y_hi'=2,'z'=8] {'x','y_lo'}, dimensions={0} | all-to-all | bytes 2097152 | tf_op jit(solution)/shard_map/all_to_all | solution.py:398
  135.8 5.6 %collective-permute-start.2 = (f32[256,1024]{1,0:T(8,128)S(1)}, f32[256,1024]{1,0:T(8,128)}, u32[]{:S(2)}, u32[]{:S(2)}) collective-permute-start(f32[256,1024]{1,0:T(8,128)S(1)} %bitcast.13), channel_id=1, source_target_pairs={{0,16},{16,0},{1,17},{17,1},{2,18},{18,2},{3,19},{19,3},{4,20},{20... | collective-permute-start | bytes 3145736 | tf_op jit(solution)/shard_map/ppermute | solution.py:402
  141.5 2.2 %shard_map.38.refs_0_ = f32[896,1024]{1,0:T(8,128)S(1)} custom-call(s32[2]{0:T(128)S(1)} %pad_add_fusion.2.place_ref, bf16[896,512]{1,0:T(8,128)(2,1)S(1)} %copy-done.3, f32[256,1024]{1,0:T(8,128)S(1)} %bitcast.14), custom_call_target="tpu_custom_call" | custom-call | flops 1409286144 | bytes 8388608 | tf_op jit(solution)/shard_map/pallas_call | solution.py:379
  143.8 2.9 %shard_map.39 = f32[896,1024]{1,0:T(8,128)S(1)} custom-call(s32[2]{0:T(128)S(1)} %pad_add_fusion.place_ref, bf16[896,512]{1,0:T(8,128)(2,1)S(1)} %copy-done.3, f32[256,1024]{1,0:T(8,128)} %collective-permute-done.2.part_ref, f32[896,1024]{1,0:T(8,128)S(1)} %shard_map.38.refs_0_), custom_call_target="tpu_custom_call" | custom-call | flops 1409286144 | bytes 8388608 | tf_op jit(solution)/shard_map/pallas_call | solution.py:379
  146.7 1.8 copy-done.1
  148.5 1.4 slice.9.own_ref
  149.9 0.7 collective-permute-start.3
  150.6 2.7 %collective-permute-done.3.other_ref = f32[512,640]{1,0:T(8,128)S(1)} collective-permute-done((f32[512,640]{1,0:T(8,128)S(1)}, f32[512,640]{1,0:T(8,128)S(1)}, u32[]{:S(2)}, u32[]{:S(2)}) %collective-permute-start.3) | collective-permute-done | bytes 1310752 | tf_op jit(solution)/shard_map/ppermute | solution.py:402
  153.3 1.0 copy-done.6
  154.3 44.8 %shard_map.40.value_ref = f32[1024,1024]{1,0:T(8,128)} custom-call(s32[1]{0:T(128)} %bitcast.2.core_ref, f32[512,640]{1,0:T(8,128)} %copy-done.5, f32[512,640]{1,0:T(8,128)} %copy-done.6), custom_call_target="tpu_custom_call" | custom-call | flops 12884901888 | bytes 8388608 | tf_op jit(solution)/shard_map/pallas_call | solution.py:229
  199.1 0.2 reduce-scatter.2.cloned.1.call-done
  199.3 1.1 fusion
  200.4 2.8 %collective-permute-start.4 = (f32[56,1024]{1,0:T(8,128)S(1)}, f32[56,1024]{1,0:T(8,128)S(1)}, u32[]{:S(2)}, u32[]{:S(2)}) collective-permute-start(f32[56,1024]{1,0:T(8,128)S(1)} %get-tuple-element.31), channel_id=1, source_target_pairs={{0,8},{8,0},{1,9},{9,1},{2,10},{10,2},{3,11},{11,3},{4,12},{12,4},... | collective-permute-start | bytes 688136 | tf_op jit(solution)/shard_map/ppermute | solution.py:402
  203.3 2.2 %copy-done.2 = f32[1024,1024]{1,0:T(8,128)S(1)} copy-done((f32[1024,1024]{1,0:T(8,128)S(1)}, f32[1024,1024]{1,0:T(8,128)}, u32[]{:S(2)}) %copy-start.2) | copy-done | bytes 4194328
  205.4 1.3 shard_map.41
  206.7 1.8 collective-permute-done.4.other_ref
  208.5 2.2 %shard_map.42 = f32[56,1024]{1,0:T(8,128)} custom-call(f32[56,1024]{1,0:T(8,128)S(1)} %get-tuple-element.32.own_ref, f32[56,1024]{1,0:T(8,128)S(1)} %collective-permute-done.4.other_ref, bf16[1024,1024]{1,0:T(8,128)(2,1)S(1)} %get-tuple-element.28.high_ref, bf16[1024,1024]{1,0:T(8,128)(2,1)S(1)} %get-tuple-element.29.middle_ref, ...), custom_call_target="tpu_custom_call" | custom-call | flops 704643072 | bytes 7340032 | tf_op jit(solution)/shard_map/pallas_call | solution.py:298
  (26 shorter events, 0.6 us)
Async XLA Ops:
  6.5 1.2 copy-start
  47.2 32.9 %copy-start.4 = (bf16[256,512]{1,0:T(8,128)(2,1)S(1)}, bf16[256,512]{1,0:T(8,128)(2,1)}, u32[]{:S(2)}) copy-start(bf16[256,512]{1,0:T(8,128)(2,1)} %activations_ref.1) | copy-start | bytes 786436
  48.4 31.8 %all-to-all-start.1 = ((f32[16,16,1024]{2,1,0:T(8,128)}), f32[16,16,1024]{2,1,0:T(8,128)S(1)}, u32[]{:S(2)}, u32[]{:S(2)}) async-start(f32[16,16,1024]{2,1,0:T(8,128)} %broadcast_in_dim.6), calls=%async_computation.1 | async-start | bytes 2097152 | tf_op jit(solution)/shard_map/all_to_all | solution.py:398
  54.3 94.1 %all-gather.2.cloned.1.call-start = ((), (), s32[]{:S(2)}) async-start(), calls=%async_computation.7 | async-start | bytes 2949120 | tf_op jit(solution)/shard_map/all_gather | solution.py:420
  82.2 23.5 %collective-permute-start = (f32[256,1024]{1,0:T(8,128)}, f32[256,1024]{1,0:T(8,128)}, u32[]{:S(2)}, u32[]{:S(2)}) collective-permute-start(f32[256,1024]{1,0:T(8,128)} %get-tuple-element.19), channel_id=1, source_target_pairs={{0,16},{16,0},{1,17},{17,1},{2,18},{18,2},{3,19},{19,3},{4,20},{20... | collective-permute-start | bytes 3145736 | tf_op jit(solution)/shard_map/ppermute | solution.py:402
  85.1 2.4 %collective-permute-start.1 = (f32[64,640]{1,0:T(8,128)S(1)}, f32[64,640]{1,0:T(8,128)S(1)}, u32[]{:S(2)}, u32[]{:S(2)}) collective-permute-start(f32[64,640]{1,0:T(8,128)S(1)} %get-tuple-element.21), channel_id=1, source_target_pairs={{0,16},{16,0},{1,17},{17,1},{2,18},{18,2},{3,19},{19,3},{4,20},{20... | collective-permute-start | bytes 491528 | tf_op jit(solution)/shard_map/ppermute | solution.py:402
  107.0 92.3 %reduce-scatter.2.cloned.1.call-start = ((), (), s32[]{:S(2)}) async-start(), calls=%async_computation.8 | async-start | bytes 4128768 | tf_op jit(solution)/shard_map/reduce_scatter | solution.py:425
  122.0 19.5 %copy-start.3 = (bf16[896,512]{1,0:T(8,128)(2,1)S(1)}, bf16[896,512]{1,0:T(8,128)(2,1)}, u32[]{:S(2)}) copy-start(bf16[896,512]{1,0:T(8,128)(2,1)} %weight_ref.3) | copy-start | bytes 2752516
  135.8 8.0 %collective-permute-start.2 = (f32[256,1024]{1,0:T(8,128)S(1)}, f32[256,1024]{1,0:T(8,128)}, u32[]{:S(2)}, u32[]{:S(2)}) collective-permute-start(f32[256,1024]{1,0:T(8,128)S(1)} %bitcast.13), channel_id=1, source_target_pairs={{0,16},{16,0},{1,17},{17,1},{2,18},{18,2},{3,19},{19,3},{4,20},{20... | collective-permute-start | bytes 3145736 | tf_op jit(solution)/shard_map/ppermute | solution.py:402
  146.7 1.8 copy-start.1
  149.9 3.4 %copy-start.5 = (f32[512,640]{1,0:T(8,128)}, f32[512,640]{1,0:T(8,128)S(1)}, u32[]{:S(2)}) copy-start(f32[512,640]{1,0:T(8,128)S(1)} %slice.9.own_ref) | copy-start | bytes 3932164
  149.9 3.4 %collective-permute-start.3 = (f32[512,640]{1,0:T(8,128)S(1)}, f32[512,640]{1,0:T(8,128)S(1)}, u32[]{:S(2)}, u32[]{:S(2)}) collective-permute-start(f32[512,640]{1,0:T(8,128)S(1)} %slice.9.own_ref), channel_id=1, source_target_pairs={{0,16},{16,0},{1,17},{17,1},{2,18},{18,2},{3,19},{19,3},{4,20},{20... | collective-permute-start | bytes 3932168 | tf_op jit(solution)/shard_map/ppermute | solution.py:402
  153.3 1.0 copy-start.6
  200.4 8.1 %collective-permute-start.4 = (f32[56,1024]{1,0:T(8,128)S(1)}, f32[56,1024]{1,0:T(8,128)S(1)}, u32[]{:S(2)}, u32[]{:S(2)}) collective-permute-start(f32[56,1024]{1,0:T(8,128)S(1)} %get-tuple-element.31), channel_id=1, source_target_pairs={{0,8},{8,0},{1,9},{9,1},{2,10},{10,2},{3,11},{11,3},{4,12},{12,4},... | collective-permute-start | bytes 688136 | tf_op jit(solution)/shard_map/ppermute | solution.py:402
  203.3 2.2 %copy-start.2 = (f32[1024,1024]{1,0:T(8,128)S(1)}, f32[1024,1024]{1,0:T(8,128)}, u32[]{:S(2)}) copy-start(f32[1024,1024]{1,0:T(8,128)} %shard_map.40.value_ref) | copy-start | bytes 12582916
Sparse Core Ops, SparseCore 0:
  107.1 37.5 all-gather.1
  148.6 50.6 reduce-scatter.1

commit v5 on v4

--- a/solution.py
+++ b/solution.py
@@ -132,13 +132,13 @@
 
 
 def inverse_kernel(
-    core_ref, own_ref, other_ref, result_ref, out_ref, left_ref, right_ref, block_ref, buffer, done
+    place_ref, own_ref, other_ref, result_ref, out_ref, left_ref, right_ref, block_ref, buffer, done
 ):
     size = out_ref.shape[0]
     blocks = size // LANE
     tile = 256
     half = LANE // 2
-    core = core_ref[0]
+    core = place_ref[0]
     row = lax.broadcasted_iota(jnp.int32, (LANE, LANE), 0)
     column = lax.broadcasted_iota(jnp.int32, (LANE, LANE), 1)
     diagonal = row == column
@@ -221,10 +221,10 @@
 OUTSIDE = pl.BlockSpec(memory_space=pltpu.HBM)
 SCALARS = pl.BlockSpec(memory_space=pltpu.SMEM)
 ROOM = pltpu.CompilerParams(vmem_limit_bytes=40 * 2**20)
-MOST = pltpu.CompilerParams(vmem_limit_bytes=60 * 2**20)
-
-
-def swept(core, own, other):
+MOST = pltpu.CompilerParams(vmem_limit_bytes=58 * 2**20)
+
+
+def swept(place, own, other):
     size = 2 * own.shape[0]
     return pl.pallas_call(
         inverse_kernel,
@@ -243,7 +243,7 @@
         cost_estimate=pl.CostEstimate(
             flops=12 * size**3, bytes_accessed=8 * size**2, transcendentals=0
         ),
-    )(core, own, other)
+    )(place, own, other)
 
 
 def split_kernel(value_ref, high_ref, middle_ref, low_ref):
@@ -374,8 +374,7 @@
                 out_ref[target, columns] = value
 
 
-def cross_terms(core, y_hi, weight, part, *earlier):
-    place = jnp.stack([core, y_hi]).astype(jnp.int32)
+def cross_terms(place, weight, part, *earlier):
     return pl.pallas_call(
         cross_kernel,
         out_shape=jax.ShapeDtypeStruct((weight.shape[0], part.shape[1]), jnp.float32),
@@ -403,28 +402,31 @@
 
 
 def shards(activations, weight, basis):
-    core, y_hi, z = (lax.axis_index(name) for name in ("core", "y_hi", "z"))
+    core, y_hi, z = (lax.axis_index(name).astype(jnp.int32) for name in ("core", "y_hi", "z"))
+    activations, core, y_hi, z = lax.optimization_barrier((activations, core, y_hi, z))
     partial_value = lax.dot_general(
         activations, basis, (((1,), (1,)), ((), ())), preferred_element_type=jnp.float32
     )
     codes = exchange_gather(exchange_sum(partial_value, CH, 16), CH, 16)
-
-    here = core.astype(jnp.int32)[None]
-    place = jnp.stack([core, z]).astype(jnp.int32)
+    codes, core, y_hi, z = lax.optimization_barrier((codes, core, y_hi, z))
+    place = jnp.stack([core, z])
+    places = [jnp.stack([index, y_hi]) for index in (core, 1 - core)]
+
     own, other, gram, gram_other = partial_terms(place, codes, activations)
     gram = gram + swap(gram_other, "core")
-    own = own + swap(other, "core")
+    other = swap(other, "core")
     gram = exchange_gather(exchange_sum(gram, PLANE, 8), PLANE, 8)
     gram = jnp.concatenate([gram, gram], 1)
-    own, gram = lax.optimization_barrier((own, gram))
+    other, gram = lax.optimization_barrier((other, gram))
+    own = own + other
     gram = lax.all_gather(gram, "z", axis=0, tiled=True)
     own = exchange_gather(exchange_sum(own, PLANE, 8), PLANE, 8)
-    cross = cross_terms(core, y_hi, weight, own)
-    cross = cross_terms(1 - core, y_hi, weight, swap(own, "core"), cross)
+    cross = cross_terms(places[0], weight, own)
+    cross = cross_terms(places[1], weight, swap(own, "core"), cross)
     cross, gram = lax.optimization_barrier((cross, gram))
     cross = lax.psum_scatter(cross, "z", scatter_dimension=0, tiled=True)
     gram = gram[:, : STRIP * LANE]
-    inverse = swept(here, gram, swap(gram, "core"))
+    inverse = swept(place, gram, swap(gram, "core"))
     cross, inverse = lax.optimization_barrier((cross, inverse))
     half = cross.shape[0] // 2
     return solve(cross[:half], swap(cross[half:], "y_hi"), split_rows(inverse))

time: 218 us -> 217 us (level)
  blocking collectives: 83.9 us -> 115 us
  waiting for transfers between devices: 32.8 us -> 8.29 us
  starting transfers between devices: 18.1 us -> 11.7 us
    all_to_all x2 -> x3, blocking collectives: 21.5 us -> 52.6 us  [exchange_gather(): lax.all_to_all(copies.reshape(-1, value.shape[1]), axes, 0, 0, tiled=True)]
    all_to_all x1 -> x0, waiting for transfers between devices: 25.6 us -> none  [exchange_gather(): lax.all_to_all(copies.reshape(-1, value.shape[1]), axes, 0, 0, tiled=True)]
    all_to_all x1 -> x0, starting transfers between devices: 5.98 us -> none  [exchange_gather(): lax.all_to_all(copies.reshape(-1, value.shape[1]), axes, 0, 0, tiled=True)]
    unnamed x14 -> x16, local copies, waits for them, and re-layouts: 6.26 us -> 6.27 us
  transfers between devices with their start and end apart: 8 -> 7, of which waited for: 6 -> 4; matrix products, arithmetic and copies ran while one was open for 1% -> 2% of each run, Pallas kernels for 23% -> 24%
where the time goes in v5:
time: 217 us; the launch traced here: 216 us
  blocking collectives  115 us (53%)
  Pallas kernels  54.9 us (25%)
  between operations  13.5 us (6%)
  starting transfers between devices  11.7 us (5%)
  local copies, waits for them, and re-layouts  8.98 us (4%)
  waiting for transfers between devices  8.29 us (4%)
  other arithmetic  2.51 us (1%)
    all_to_all x3, blocking collectives, exchange_sum(): received = lax.all_to_all(value, axes, 0, 0, tiled=True)  62.5 us
    all_to_all x3, blocking collectives, exchange_gather(): lax.all_to_all(copies.reshape(-1, value.shape[1]), axes, 0, 0, tiled=True)  52.6 us
    pallas_call x1, Pallas kernels, swept(): pl.pallas_call(inverse_kernel, out_shape=jax.ShapeDtypeStruct((size, size...  44.8 us
    ppermute x5, starting transfers between devices, swap(): return lax.ppermute(value, axis, [(0, 1), (1, 0)])  11.6 us
    ppermute x5, waiting for transfers between devices, swap(): return lax.ppermute(value, axis, [(0, 1), (1, 0)])  8.23 us
    unnamed x16, local copies, waits for them, and re-layouts  6.27 us
    pallas_call x2, Pallas kernels, cross_terms(): pl.pallas_call(cross_kernel, out_shape=jax.ShapeDtypeStruct((weight.shape...  5.07 us
  transfers between devices with their start and end apart: 7, of which 4 were waited for; matrix products, arithmetic and copies ran while one was open for 2% of the time, Pallas kernels for 24%

profile of v5, /device:TPU:1, one launch (start us, length us, event | category | flops | bytes accessed | tf_op | source)
XLA Modules:
  0.0 216.4 jit_solution(12710401283187021622)
XLA Ops:
  6.5 1.2 copy-done
  7.8 1.4 fusion.1
  9.2 38.0 %all_to_all.53 = f32[16,16,1024]{2,1,0:T(8,128)S(1)} all-to-all(f32[16,16,1024]{2,1,0:T(8,128)S(1)} %bitcast.17), channel_id=1, replica_groups=mesh['x'=4,'y_lo'=2,'core'=2,'y_hi'=2,'z'=8] {'y_hi','z'}, dimensions={0} | all-to-all | bytes 2097152 | tf_op jit(solution)/shard_map/all_to_all | solution.py:391
  47.3 0.1 broadcast_in_dim.6
  47.4 31.1 %all_to_all.54 = f32[16,16,1024]{2,1,0:T(8,128)S(1)} all-to-all(f32[16,16,1024]{2,1,0:T(8,128)S(1)} %broadcast_in_dim.6), channel_id=1, replica_groups=mesh['x'=4,'y_lo'=2,'core'=2,'y_hi'=2,'z'=8] {'y_hi','z'}, dimensions={0} | all-to-all | bytes 2097152 | tf_op jit(solution)/shard_map/all_to_all | solution.py:397
  78.5 0.1 pad_add_fusion.1.place_ref
  78.6 1.6 shard_map.37
  80.1 3.6 %collective-permute-start = (f32[256,1024]{1,0:T(8,128)S(1)}, f32[256,1024]{1,0:T(8,128)}, u32[]{:S(2)}, u32[]{:S(2)}) collective-permute-start(f32[256,1024]{1,0:T(8,128)S(1)} %get-tuple-element.35), channel_id=1, source_target_pairs={{0,16},{16,0},{1,17},{17,1},{2,18},{18,2},{3,19},{19,3},{4,20},{20... | collective-permute-start | bytes 3145736 | tf_op jit(solution)/shard_map/ppermute | solution.py:401
  83.7 0.1 collective-permute-start.1
  83.8 2.3 %collective-permute-done.1 = f32[64,640]{1,0:T(8,128)S(1)} collective-permute-done((f32[64,640]{1,0:T(8,128)S(1)}, f32[64,640]{1,0:T(8,128)S(1)}, u32[]{:S(2)}, u32[]{:S(2)}) %collective-permute-start.1) | collective-permute-done | bytes 163872 | tf_op jit(solution)/shard_map/ppermute | solution.py:401
  86.1 9.5 %all_to_all.55 = f32[8,8,640]{2,1,0:T(8,128)S(1)} all-to-all(f32[8,8,640]{2,1,0:T(8,128)S(1)} %add_bitcast_fusion), channel_id=1, replica_groups=mesh['x'=4,'y_lo'=2,'core'=2,'y_hi'=2,'z'=8] {'x','y_lo'}, dimensions={0} | all-to-all | bytes 327680 | tf_op jit(solution)/shard_map/all_to_all | solution.py:391
  95.7 7.9 %all_to_all.56 = f32[8,8,640]{2,1,0:T(8,128)S(1)} all-to-all(f32[8,8,640]{2,1,0:T(8,128)S(1)} %broadcast_in_dim.7), channel_id=1, replica_groups=mesh['x'=4,'y_lo'=2,'core'=2,'y_hi'=2,'z'=8] {'x','y_lo'}, dimensions={0} | all-to-all | bytes 327680 | tf_op jit(solution)/shard_map/all_to_all | solution.py:397
  103.6 0.8 pad_maximum_fusion
  104.4 1.4 add.9
  105.8 15.0 %all_to_all.57 = f32[8,32,1024]{2,1,0:T(8,128)S(1)} all-to-all(f32[8,32,1024]{2,1,0:T(8,128)S(1)} %bitcast.16), channel_id=1, replica_groups=mesh['x'=4,'y_lo'=2,'core'=2,'y_hi'=2,'z'=8] {'x','y_lo'}, dimensions={0} | all-to-all | bytes 2097152 | tf_op jit(solution)/shard_map/all_to_all | solution.py:391
  120.8 0.1 broadcast_in_dim.8
  120.9 13.6 %all_to_all.58 = f32[8,32,1024]{2,1,0:T(8,128)S(1)} all-to-all(f32[8,32,1024]{2,1,0:T(8,128)S(1)} %broadcast_in_dim.8), channel_id=1, replica_groups=mesh['x'=4,'y_lo'=2,'core'=2,'y_hi'=2,'z'=8] {'x','y_lo'}, dimensions={0} | all-to-all | bytes 2097152 | tf_op jit(solution)/shard_map/all_to_all | solution.py:397
  134.5 5.6 %collective-permute-start.2 = (f32[256,1024]{1,0:T(8,128)S(1)}, f32[256,1024]{1,0:T(8,128)}, u32[]{:S(2)}, u32[]{:S(2)}) collective-permute-start(f32[256,1024]{1,0:T(8,128)S(1)} %bitcast.13), channel_id=1, source_target_pairs={{0,16},{16,0},{1,17},{17,1},{2,18},{18,2},{3,19},{19,3},{4,20},{20... | collective-permute-start | bytes 3145736 | tf_op jit(solution)/shard_map/ppermute | solution.py:401
  140.2 2.2 %shard_map.38.refs_0_ = f32[896,1024]{1,0:T(8,128)S(1)} custom-call(s32[2]{0:T(128)S(1)} %pad_add_fusion.2.place_ref, bf16[896,512]{1,0:T(8,128)(2,1)S(1)} %copy-done.3, f32[256,1024]{1,0:T(8,128)S(1)} %bitcast.14), custom_call_target="tpu_custom_call" | custom-call | flops 1409286144 | bytes 8388608 | tf_op jit(solution)/shard_map/pallas_call | solution.py:378
  142.5 2.9 %shard_map.39 = f32[896,1024]{1,0:T(8,128)S(1)} custom-call(s32[2]{0:T(128)S(1)} %pad_add_fusion.place_ref, bf16[896,512]{1,0:T(8,128)(2,1)S(1)} %copy-done.3, f32[256,1024]{1,0:T(8,128)} %collective-permute-done.2.part_ref, f32[896,1024]{1,0:T(8,128)S(1)} %shard_map.38.refs_0_), custom_call_target="tpu_custom_call" | custom-call | flops 1409286144 | bytes 8388608 | tf_op jit(solution)/shard_map/pallas_call | solution.py:378
  145.4 1.8 copy-done.1
  147.2 1.4 slice.9.own_ref
  148.7 0.7 collective-permute-start.3
  149.4 2.7 %collective-permute-done.3.other_ref = f32[512,640]{1,0:T(8,128)S(1)} collective-permute-done((f32[512,640]{1,0:T(8,128)S(1)}, f32[512,640]{1,0:T(8,128)S(1)}, u32[]{:S(2)}, u32[]{:S(2)}) %collective-permute-start.3) | collective-permute-done | bytes 1310752 | tf_op jit(solution)/shard_map/ppermute | solution.py:401
  152.0 1.0 copy-done.7
  153.1 44.8 %shard_map.40.value_ref = f32[1024,1024]{1,0:T(8,128)} custom-call(s32[2]{0:T(128)} %copy-done.5, f32[512,640]{1,0:T(8,128)} %copy-done.6, f32[512,640]{1,0:T(8,128)} %copy-done.7), custom_call_target="tpu_custom_call" | custom-call | flops 12884901888 | bytes 8388608 | tf_op jit(solution)/shard_map/pallas_call | solution.py:229
  197.9 1.1 fusion
  199.0 1.7 collective-permute-start.4
  200.6 2.2 %copy-done.2 = f32[1024,1024]{1,0:T(8,128)S(1)} copy-done((f32[1024,1024]{1,0:T(8,128)S(1)}, f32[1024,1024]{1,0:T(8,128)}, u32[]{:S(2)}) %copy-start.2) | copy-done | bytes 4194328
  202.8 1.3 shard_map.41
  204.1 3.2 %collective-permute-done.4.other_ref = f32[56,1024]{1,0:T(8,128)S(1)} collective-permute-done((f32[56,1024]{1,0:T(8,128)S(1)}, f32[56,1024]{1,0:T(8,128)S(1)}, u32[]{:S(2)}, u32[]{:S(2)}) %collective-permute-start.4) | collective-permute-done | bytes 229408 | tf_op jit(solution)/shard_map/ppermute | solution.py:401
  207.3 2.2 %shard_map.42 = f32[56,1024]{1,0:T(8,128)} custom-call(f32[56,1024]{1,0:T(8,128)S(1)} %get-tuple-element.48.own_ref, f32[56,1024]{1,0:T(8,128)S(1)} %collective-permute-done.4.other_ref, bf16[1024,1024]{1,0:T(8,128)(2,1)S(1)} %get-tuple-element.44.high_ref, bf16[1024,1024]{1,0:T(8,128)(2,1)S(1)} %get-tuple-element.45.middle_ref, ...), custom_call_target="tpu_custom_call" | custom-call | flops 704643072 | bytes 7340032 | tf_op jit(solution)/shard_map/pallas_call | solution.py:298
  (27 shorter events, 0.5 us)
Async XLA Ops:
  6.5 1.2 copy-start
  6.5 140.7 %all-gather.2.cloned.1.call-start = ((), (), s32[]{:S(2)}) async-start(), calls=%async_computation.7 | async-start | bytes 2949120 | tf_op jit(solution)/shard_map/all_gather | solution.py:422
  47.2 31.4 %copy-start.4 = (bf16[256,512]{1,0:T(8,128)(2,1)S(1)}, bf16[256,512]{1,0:T(8,128)(2,1)}, u32[]{:S(2)}) copy-start(bf16[256,512]{1,0:T(8,128)(2,1)} %activations_ref) | copy-start | bytes 786436
  78.6 25.8 %copy-start.5 = (s32[2]{0:T(128)}, s32[2]{0:T(128)S(1)}, u32[]{:S(2)}) copy-start(s32[2]{0:T(128)S(1)} %pad_add_fusion.1.place_ref) | copy-start | bytes 28
  80.1 24.2 %collective-permute-start = (f32[256,1024]{1,0:T(8,128)S(1)}, f32[256,1024]{1,0:T(8,128)}, u32[]{:S(2)}, u32[]{:S(2)}) collective-permute-start(f32[256,1024]{1,0:T(8,128)S(1)} %get-tuple-element.35), channel_id=1, source_target_pairs={{0,16},{16,0},{1,17},{17,1},{2,18},{18,2},{3,19},{19,3},{4,20},{20... | collective-permute-start | bytes 3145736 | tf_op jit(solution)/shard_map/ppermute | solution.py:401
  83.7 2.4 %collective-permute-start.1 = (f32[64,640]{1,0:T(8,128)S(1)}, f32[64,640]{1,0:T(8,128)S(1)}, u32[]{:S(2)}, u32[]{:S(2)}) collective-permute-start(f32[64,640]{1,0:T(8,128)S(1)} %get-tuple-element.37), channel_id=1, source_target_pairs={{0,16},{16,0},{1,17},{17,1},{2,18},{18,2},{3,19},{19,3},{4,20},{20... | collective-permute-start | bytes 491528 | tf_op jit(solution)/shard_map/ppermute | solution.py:401
  104.4 93.5 %reduce-scatter.2.cloned.1.call-start = ((), (), s32[]{:S(2)}) async-start(), calls=%async_computation.8 | async-start | bytes 4128768 | tf_op jit(solution)/shard_map/reduce_scatter | solution.py:427
  120.8 19.5 %copy-start.3 = (bf16[896,512]{1,0:T(8,128)(2,1)S(1)}, bf16[896,512]{1,0:T(8,128)(2,1)}, u32[]{:S(2)}) copy-start(bf16[896,512]{1,0:T(8,128)(2,1)} %weight_ref.3) | copy-start | bytes 2752516
  134.5 8.0 %collective-permute-start.2 = (f32[256,1024]{1,0:T(8,128)S(1)}, f32[256,1024]{1,0:T(8,128)}, u32[]{:S(2)}, u32[]{:S(2)}) collective-permute-start(f32[256,1024]{1,0:T(8,128)S(1)} %bitcast.13), channel_id=1, source_target_pairs={{0,16},{16,0},{1,17},{17,1},{2,18},{18,2},{3,19},{19,3},{4,20},{20... | collective-permute-start | bytes 3145736 | tf_op jit(solution)/shard_map/ppermute | solution.py:401
  145.4 1.8 copy-start.1
  148.6 3.4 %copy-start.6 = (f32[512,640]{1,0:T(8,128)}, f32[512,640]{1,0:T(8,128)S(1)}, u32[]{:S(2)}) copy-start(f32[512,640]{1,0:T(8,128)S(1)} %slice.9.own_ref) | copy-start | bytes 3932164
  148.7 3.4 %collective-permute-start.3 = (f32[512,640]{1,0:T(8,128)S(1)}, f32[512,640]{1,0:T(8,128)S(1)}, u32[]{:S(2)}, u32[]{:S(2)}) collective-permute-start(f32[512,640]{1,0:T(8,128)S(1)} %slice.9.own_ref), channel_id=1, source_target_pairs={{0,16},{16,0},{1,17},{17,1},{2,18},{18,2},{3,19},{19,3},{4,20},{20... | collective-permute-start | bytes 3932168 | tf_op jit(solution)/shard_map/ppermute | solution.py:401
  152.0 1.0 copy-start.7
  199.0 8.4 %collective-permute-start.4 = (f32[56,1024]{1,0:T(8,128)S(1)}, f32[56,1024]{1,0:T(8,128)S(1)}, u32[]{:S(2)}, u32[]{:S(2)}) collective-permute-start(f32[56,1024]{1,0:T(8,128)S(1)} %get-tuple-element.47), channel_id=1, source_target_pairs={{0,8},{8,0},{1,9},{9,1},{2,10},{10,2},{3,11},{11,3},{4,12},{12,4},... | collective-permute-start | bytes 688136 | tf_op jit(solution)/shard_map/ppermute | solution.py:401
  200.6 2.2 %copy-start.2 = (f32[1024,1024]{1,0:T(8,128)S(1)}, f32[1024,1024]{1,0:T(8,128)}, u32[]{:S(2)}) copy-start(f32[1024,1024]{1,0:T(8,128)} %shard_map.40.value_ref) | copy-start | bytes 12582916
Sparse Core Ops, SparseCore 0:
  104.5 37.4 all-gather.1
  147.4 49.3 reduce-scatter.1

commit v6 on v5

--- a/solution.py
+++ b/solution.py
@@ -176,7 +176,15 @@
             right_ref[:, columns] = right_parts(scaled)
             out_ref[here, columns] = scaled
 
-    def step(k, carry):
+    end = size - LANE
+    copies = []
+
+    def send(rows):
+        copy = pltpu.make_async_copy(out_ref.at[rows], result_ref.at[rows], done.at[len(copies)])
+        copy.start()
+        copies.append(copy)
+
+    def step(k, last):
         here = pl.ds(pl.multiple_of(k * LANE, LANE), LANE)
         after = pl.ds(pl.multiple_of((k + 1) * LANE, LANE), LANE)
         inverse = block_ref[...]
@@ -200,21 +208,23 @@
             out_ref[rows, columns] = out_ref[rows, columns] - product(
                 left_ref[rows, :], right_ref[:, columns]
             )
+            if last and n == size // tile - 1:
+                send(slice(m * tile, min((m + 1) * tile, end)))
 
         keep(invert_block(following, buffer, update))
+
+    def early_step(k, carry):
+        step(k, False)
         return carry
 
-    lax.fori_loop(0, blocks - 1, step, 0)
-    end = size - LANE
-    upper = pltpu.make_async_copy(out_ref.at[:end], result_ref.at[:end], done.at[0])
-    upper.start()
+    lax.fori_loop(0, blocks - 2, early_step, 0)
+    step(blocks - 2, True)
     inverse = block_ref[...]
     pivot_rows(slice(end, size), inverse)
     out_ref[end:, end:] = inverse
-    lower = pltpu.make_async_copy(out_ref.at[end:], result_ref.at[end:], done.at[1])
-    lower.start()
-    upper.wait()
-    lower.wait()
+    send(slice(end, size))
+    for copy in copies:
+        copy.wait()
 
 
 WHOLE = pl.BlockSpec(memory_space=pltpu.VMEM)
@@ -237,7 +247,7 @@
             pltpu.VMEM((6 * LANE, size), jnp.bfloat16),
             pltpu.VMEM((LANE, LANE), jnp.float32),
             pltpu.VMEM((2 * (SUB + 2) * SUB, LANE), jnp.float32),
-            pltpu.SemaphoreType.DMA((2,)),
+            pltpu.SemaphoreType.DMA((5,)),
         ],
         compiler_params=MOST,
         cost_estimate=pl.CostEstimate(

time: 217 us -> 216 us (level)
  transfers between devices with their start and end apart: 7 -> 7, of which waited for: 4 -> 4; matrix products, arithmetic and copies ran while one was open for 2% -> 2% of each run, Pallas kernels for 24% -> 23%
where the time goes in v6:
time: 216 us; the launch traced here: 215 us
  blocking collectives  115 us (53%)
  Pallas kernels  54.1 us (25%)
  between operations  13.5 us (6%)
  starting transfers between devices  12.5 us (6%)
  local copies, waits for them, and re-layouts  8.98 us (4%)
  waiting for transfers between devices  7.23 us (3%)
  other arithmetic  2.51 us (1%)
    all_to_all x3, blocking collectives, exchange_sum(): received = lax.all_to_all(value, axes, 0, 0, tiled=True)  62.5 us
    all_to_all x3, blocking collectives, exchange_gather(): lax.all_to_all(copies.reshape(-1, value.shape[1]), axes, 0, 0, tiled=True)  52.6 us
    pallas_call x1, Pallas kernels, swept(): pl.pallas_call(inverse_kernel, out_shape=jax.ShapeDtypeStruct((size, size...  44 us
    ppermute x5, starting transfers between devices, swap(): return lax.ppermute(value, axis, [(0, 1), (1, 0)])  12.4 us
    ppermute x5, waiting for transfers between devices, swap(): return lax.ppermute(value, axis, [(0, 1), (1, 0)])  7.17 us
    unnamed x16, local copies, waits for them, and re-layouts  6.27 us
    pallas_call x2, Pallas kernels, cross_terms(): pl.pallas_call(cross_kernel, out_shape=jax.ShapeDtypeStruct((weight.shape...  5.07 us
  transfers between devices with their start and end apart: 7, of which 4 were waited for; matrix products, arithmetic and copies ran while one was open for 2% of the time, Pallas kernels for 23%

profile of v6, /device:TPU:1, one launch (start us, length us, event | category | flops | bytes accessed | tf_op | source)
XLA Modules:
  0.0 215.4 jit_solution(10103780331427262890)
XLA Ops:
  6.5 1.2 copy-done
  7.8 1.4 fusion.1
  9.2 38.0 %all_to_all.53 = f32[16,16,1024]{2,1,0:T(8,128)S(1)} all-to-all(f32[16,16,1024]{2,1,0:T(8,128)S(1)} %bitcast.17), channel_id=1, replica_groups=mesh['x'=4,'y_lo'=2,'core'=2,'y_hi'=2,'z'=8] {'y_hi','z'}, dimensions={0} | all-to-all | bytes 2097152 | tf_op jit(solution)/shard_map/all_to_all | solution.py:401
  47.3 0.1 broadcast_in_dim.6
  47.4 31.1 %all_to_all.54 = f32[16,16,1024]{2,1,0:T(8,128)S(1)} all-to-all(f32[16,16,1024]{2,1,0:T(8,128)S(1)} %broadcast_in_dim.6), channel_id=1, replica_groups=mesh['x'=4,'y_lo'=2,'core'=2,'y_hi'=2,'z'=8] {'y_hi','z'}, dimensions={0} | all-to-all | bytes 2097152 | tf_op jit(solution)/shard_map/all_to_all | solution.py:407
  78.5 0.1 pad_add_fusion.1.place_ref
  78.6 1.6 shard_map.37
  80.1 3.6 %collective-permute-start = (f32[256,1024]{1,0:T(8,128)S(1)}, f32[256,1024]{1,0:T(8,128)}, u32[]{:S(2)}, u32[]{:S(2)}) collective-permute-start(f32[256,1024]{1,0:T(8,128)S(1)} %get-tuple-element.35), channel_id=1, source_target_pairs={{0,16},{16,0},{1,17},{17,1},{2,18},{18,2},{3,19},{19,3},{4,20},{20... | collective-permute-start | bytes 3145736 | tf_op jit(solution)/shard_map/ppermute | solution.py:411
  83.7 0.1 collective-permute-start.1
  83.8 2.3 %collective-permute-done.1 = f32[64,640]{1,0:T(8,128)S(1)} collective-permute-done((f32[64,640]{1,0:T(8,128)S(1)}, f32[64,640]{1,0:T(8,128)S(1)}, u32[]{:S(2)}, u32[]{:S(2)}) %collective-permute-start.1) | collective-permute-done | bytes 163872 | tf_op jit(solution)/shard_map/ppermute | solution.py:411
  86.1 9.5 %all_to_all.55 = f32[8,8,640]{2,1,0:T(8,128)S(1)} all-to-all(f32[8,8,640]{2,1,0:T(8,128)S(1)} %add_bitcast_fusion), channel_id=1, replica_groups=mesh['x'=4,'y_lo'=2,'core'=2,'y_hi'=2,'z'=8] {'x','y_lo'}, dimensions={0} | all-to-all | bytes 327680 | tf_op jit(solution)/shard_map/all_to_all | solution.py:401
  95.7 7.9 %all_to_all.56 = f32[8,8,640]{2,1,0:T(8,128)S(1)} all-to-all(f32[8,8,640]{2,1,0:T(8,128)S(1)} %broadcast_in_dim.7), channel_id=1, replica_groups=mesh['x'=4,'y_lo'=2,'core'=2,'y_hi'=2,'z'=8] {'x','y_lo'}, dimensions={0} | all-to-all | bytes 327680 | tf_op jit(solution)/shard_map/all_to_all | solution.py:407
  103.6 0.8 pad_maximum_fusion
  104.4 1.4 add.9
  105.8 15.0 %all_to_all.57 = f32[8,32,1024]{2,1,0:T(8,128)S(1)} all-to-all(f32[8,32,1024]{2,1,0:T(8,128)S(1)} %bitcast.16), channel_id=1, replica_groups=mesh['x'=4,'y_lo'=2,'core'=2,'y_hi'=2,'z'=8] {'x','y_lo'}, dimensions={0} | all-to-all | bytes 2097152 | tf_op jit(solution)/shard_map/all_to_all | solution.py:401
  120.8 0.1 broadcast_in_dim.8
  120.9 13.6 %all_to_all.58 = f32[8,32,1024]{2,1,0:T(8,128)S(1)} all-to-all(f32[8,32,1024]{2,1,0:T(8,128)S(1)} %broadcast_in_dim.8), channel_id=1, replica_groups=mesh['x'=4,'y_lo'=2,'core'=2,'y_hi'=2,'z'=8] {'x','y_lo'}, dimensions={0} | all-to-all | bytes 2097152 | tf_op jit(solution)/shard_map/all_to_all | solution.py:407
  134.5 5.6 %collective-permute-start.2 = (f32[256,1024]{1,0:T(8,128)S(1)}, f32[256,1024]{1,0:T(8,128)}, u32[]{:S(2)}, u32[]{:S(2)}) collective-permute-start(f32[256,1024]{1,0:T(8,128)S(1)} %bitcast.13), channel_id=1, source_target_pairs={{0,16},{16,0},{1,17},{17,1},{2,18},{18,2},{3,19},{19,3},{4,20},{20... | collective-permute-start | bytes 3145736 | tf_op jit(solution)/shard_map/ppermute | solution.py:411
  140.2 2.2 %shard_map.38.refs_0_ = f32[896,1024]{1,0:T(8,128)S(1)} custom-call(s32[2]{0:T(128)S(1)} %pad_add_fusion.2.place_ref, bf16[896,512]{1,0:T(8,128)(2,1)S(1)} %copy-done.3, f32[256,1024]{1,0:T(8,128)S(1)} %bitcast.14), custom_call_target="tpu_custom_call" | custom-call | flops 1409286144 | bytes 8388608 | tf_op jit(solution)/shard_map/pallas_call | solution.py:388
  142.5 2.9 %shard_map.39 = f32[896,1024]{1,0:T(8,128)S(1)} custom-call(s32[2]{0:T(128)S(1)} %pad_add_fusion.place_ref, bf16[896,512]{1,0:T(8,128)(2,1)S(1)} %copy-done.3, f32[256,1024]{1,0:T(8,128)} %collective-permute-done.2.part_ref, f32[896,1024]{1,0:T(8,128)S(1)} %shard_map.38.refs_0_), custom_call_target="tpu_custom_call" | custom-call | flops 1409286144 | bytes 8388608 | tf_op jit(solution)/shard_map/pallas_call | solution.py:388
  145.4 1.8 copy-done.1
  147.2 1.4 slice.9.own_ref
  148.7 0.5 collective-permute-start.3
  149.2 2.7 %collective-permute-done.3.other_ref = f32[512,640]{1,0:T(8,128)S(1)} collective-permute-done((f32[512,640]{1,0:T(8,128)S(1)}, f32[512,640]{1,0:T(8,128)S(1)}, u32[]{:S(2)}, u32[]{:S(2)}) %collective-permute-start.3) | collective-permute-done | bytes 1310752 | tf_op jit(solution)/shard_map/ppermute | solution.py:411
  151.8 1.0 copy-done.7
  152.9 44.0 %shard_map.40.value_ref = f32[1024,1024]{1,0:T(8,128)} custom-call(s32[2]{0:T(128)} %copy-done.5, f32[512,640]{1,0:T(8,128)} %copy-done.6, f32[512,640]{1,0:T(8,128)} %copy-done.7), custom_call_target="tpu_custom_call" | custom-call | flops 12884901888 | bytes 8388608 | tf_op jit(solution)/shard_map/pallas_call | solution.py:239
  196.9 1.1 fusion
  198.0 2.7 %collective-permute-start.4 = (f32[56,1024]{1,0:T(8,128)S(1)}, f32[56,1024]{1,0:T(8,128)S(1)}, u32[]{:S(2)}, u32[]{:S(2)}) collective-permute-start(f32[56,1024]{1,0:T(8,128)S(1)} %get-tuple-element.47), channel_id=1, source_target_pairs={{0,8},{8,0},{1,9},{9,1},{2,10},{10,2},{3,11},{11,3},{4,12},{12,4},... | collective-permute-start | bytes 688136 | tf_op jit(solution)/shard_map/ppermute | solution.py:411
  200.7 2.2 %copy-done.2 = f32[1024,1024]{1,0:T(8,128)S(1)} copy-done((f32[1024,1024]{1,0:T(8,128)S(1)}, f32[1024,1024]{1,0:T(8,128)}, u32[]{:S(2)}) %copy-start.2) | copy-done | bytes 4194328
  202.9 1.3 shard_map.41
  204.2 2.1 collective-permute-done.4.other_ref
  206.3 2.2 %shard_map.42 = f32[56,1024]{1,0:T(8,128)} custom-call(f32[56,1024]{1,0:T(8,128)S(1)} %get-tuple-element.48.own_ref, f32[56,1024]{1,0:T(8,128)S(1)} %collective-permute-done.4.other_ref, bf16[1024,1024]{1,0:T(8,128)(2,1)S(1)} %get-tuple-element.44.high_ref, bf16[1024,1024]{1,0:T(8,128)(2,1)S(1)} %get-tuple-element.45.middle_ref, ...), custom_call_target="tpu_custom_call" | custom-call | flops 704643072 | bytes 7340032 | tf_op jit(solution)/shard_map/pallas_call | solution.py:308
  (27 shorter events, 0.5 us)
Async XLA Ops:
  6.5 1.2 copy-start
  6.5 140.7 %all-gather.2.cloned.1.call-start = ((), (), s32[]{:S(2)}) async-start(), calls=%async_computation.7 | async-start | bytes 2949120 | tf_op jit(solution)/shard_map/all_gather | solution.py:432
  47.2 31.4 %copy-start.4 = (bf16[256,512]{1,0:T(8,128)(2,1)S(1)}, bf16[256,512]{1,0:T(8,128)(2,1)}, u32[]{:S(2)}) copy-start(bf16[256,512]{1,0:T(8,128)(2,1)} %activations_ref) | copy-start | bytes 786436
  78.6 25.8 %copy-start.5 = (s32[2]{0:T(128)}, s32[2]{0:T(128)S(1)}, u32[]{:S(2)}) copy-start(s32[2]{0:T(128)S(1)} %pad_add_fusion.1.place_ref) | copy-start | bytes 28
  80.1 24.2 %collective-permute-start = (f32[256,1024]{1,0:T(8,128)S(1)}, f32[256,1024]{1,0:T(8,128)}, u32[]{:S(2)}, u32[]{:S(2)}) collective-permute-start(f32[256,1024]{1,0:T(8,128)S(1)} %get-tuple-element.35), channel_id=1, source_target_pairs={{0,16},{16,0},{1,17},{17,1},{2,18},{18,2},{3,19},{19,3},{4,20},{20... | collective-permute-start | bytes 3145736 | tf_op jit(solution)/shard_map/ppermute | solution.py:411
  83.7 2.4 %collective-permute-start.1 = (f32[64,640]{1,0:T(8,128)S(1)}, f32[64,640]{1,0:T(8,128)S(1)}, u32[]{:S(2)}, u32[]{:S(2)}) collective-permute-start(f32[64,640]{1,0:T(8,128)S(1)} %get-tuple-element.37), channel_id=1, source_target_pairs={{0,16},{16,0},{1,17},{17,1},{2,18},{18,2},{3,19},{19,3},{4,20},{20... | collective-permute-start | bytes 491528 | tf_op jit(solution)/shard_map/ppermute | solution.py:411
  104.4 92.5 %reduce-scatter.2.cloned.1.call-start = ((), (), s32[]{:S(2)}) async-start(), calls=%async_computation.8 | async-start | bytes 4128768 | tf_op jit(solution)/shard_map/reduce_scatter | solution.py:437
  120.8 19.5 %copy-start.3 = (bf16[896,512]{1,0:T(8,128)(2,1)S(1)}, bf16[896,512]{1,0:T(8,128)(2,1)}, u32[]{:S(2)}) copy-start(bf16[896,512]{1,0:T(8,128)(2,1)} %weight_ref.3) | copy-start | bytes 2752516
  134.5 8.0 %collective-permute-start.2 = (f32[256,1024]{1,0:T(8,128)S(1)}, f32[256,1024]{1,0:T(8,128)}, u32[]{:S(2)}, u32[]{:S(2)}) collective-permute-start(f32[256,1024]{1,0:T(8,128)S(1)} %bitcast.13), channel_id=1, source_target_pairs={{0,16},{16,0},{1,17},{17,1},{2,18},{18,2},{3,19},{19,3},{4,20},{20... | collective-permute-start | bytes 3145736 | tf_op jit(solution)/shard_map/ppermute | solution.py:411
  145.4 1.8 copy-start.1
  148.6 3.2 %copy-start.6 = (f32[512,640]{1,0:T(8,128)}, f32[512,640]{1,0:T(8,128)S(1)}, u32[]{:S(2)}) copy-start(f32[512,640]{1,0:T(8,128)S(1)} %slice.9.own_ref) | copy-start | bytes 3932164
  148.7 3.2 %collective-permute-start.3 = (f32[512,640]{1,0:T(8,128)S(1)}, f32[512,640]{1,0:T(8,128)S(1)}, u32[]{:S(2)}, u32[]{:S(2)}) collective-permute-start(f32[512,640]{1,0:T(8,128)S(1)} %slice.9.own_ref), channel_id=1, source_target_pairs={{0,16},{16,0},{1,17},{17,1},{2,18},{18,2},{3,19},{19,3},{4,20},{20... | collective-permute-start | bytes 3932168 | tf_op jit(solution)/shard_map/ppermute | solution.py:411
  151.8 1.0 copy-start.7
  198.0 8.3 %collective-permute-start.4 = (f32[56,1024]{1,0:T(8,128)S(1)}, f32[56,1024]{1,0:T(8,128)S(1)}, u32[]{:S(2)}, u32[]{:S(2)}) collective-permute-start(f32[56,1024]{1,0:T(8,128)S(1)} %get-tuple-element.47), channel_id=1, source_target_pairs={{0,8},{8,0},{1,9},{9,1},{2,10},{10,2},{3,11},{11,3},{4,12},{12,4},... | collective-permute-start | bytes 688136 | tf_op jit(solution)/shard_map/ppermute | solution.py:411
  200.7 2.2 %copy-start.2 = (f32[1024,1024]{1,0:T(8,128)S(1)}, f32[1024,1024]{1,0:T(8,128)}, u32[]{:S(2)}) copy-start(f32[1024,1024]{1,0:T(8,128)} %shard_map.40.value_ref) | copy-start | bytes 12582916
Sparse Core Ops, SparseCore 0:
  104.5 37.4 all-gather.1
  147.4 49.3 reduce-scatter.1
